TPU v7x, 32 devices: a whole 2x2x4 slice. The times are simulated.
32 devices in a mesh: wide: 8 (over z, core), tall: 4 (over y, x).
Axes of the slice: x: 2, y: 2, z: 4, core: 2. Of those that a mesh axis runs over, the one named last changes fastest.
Arguments:
- initial: float32 [16384, 16384], P(('wide', 'tall')), as said below
- child_tiles: float32 [1024, 128, 128], P(('wide', 'tall')), may hold values from -0.75 to 0.75
- child_targets: int32 [1024, 2], P(('wide', 'tall')), may hold values from 0 to 127, as said below
Outputs:
- front: float32 [16384, 16384], P('tall', 'wide')
Inputs may be any that keep to these rules, and one draw needn't show every extreme that they name: initial is symmetric, and assembled with its lower triangle mirrored is positive definite. `child_targets`: tile t * 8 + k of a device (t < 4, k < 8) lands on a block whose rows lie in the 512 rows of initial held by device g * 4 + t, g being the sender's index along wide; such a block's grid owner is the device at tall index (block row * 128 // 512) mod 4 and wide index (block column * 128 // 512) mod 8; the 8 tiles of one device with the same t go to 8 different grid owners, so one device sends at most one tile to one owner; in every grid row some owner gets one tile from every device.
All inputs are finite; a program needn't handle non-finite values.
Results may differ from a plain program's by a relative error of at most 0.0003.
Values sent between devices are 32-bit elements; how exact they have to be, the bound alone decides.
No kernel may reach another device: no remote copies, remote signals or barrier semaphores. Data moves between devices by JAX's collectives and lax.ppermute only.
A program may use at most 256 MiB of HBM per device.

v0:
```python
import jax
import jax.numpy as jnp
import numpy as np
from jax import lax
from jax.sharding import PartitionSpec as P

PANEL = 512
PANELS = 2


full_precision = lax.Precision.HIGHEST


def from_root(value, axis, source):
    kept = jnp.where(lax.axis_index(axis) == source, value, 0).astype(value.dtype)
    return lax.psum(kept, axis)


def add_blocks(base, tiles, block_index, tile_edge):
    base_rows, base_cols = base.shape
    row_count = base_rows // tile_edge
    col_count = base_cols // tile_edge
    slot_ids = jnp.arange(row_count * col_count, dtype=jnp.int32)
    selector = (slot_ids[:, None] == block_index[None, :]).astype(jnp.float32)
    summed = jnp.dot(selector, tiles, precision=full_precision, preferred_element_type=jnp.float32)
    summed = summed.reshape(row_count, col_count, tile_edge, tile_edge).transpose(0, 2, 1, 3)
    return base + summed.reshape(base_rows, base_cols)


def relayout(slab, wide_size, panel_width):
    slab_rows, front_order = slab.shape
    col_tiles = front_order // (panel_width * wide_size)
    pieces_out = slab.reshape(slab_rows, col_tiles, wide_size, panel_width)
    arrived = lax.all_to_all(pieces_out, "wide", split_axis=2, concat_axis=0, tiled=True)
    return arrived.reshape(wide_size * slab_rows, col_tiles * panel_width)


def share_strip(front_local, panel_at, panel_width):
    wide_size = lax.axis_size("wide")
    home_tile = panel_at // wide_size
    column_piece = lax.slice_in_dim(
        front_local, home_tile * panel_width, (home_tile + 1) * panel_width, axis=1
    )
    return from_root(column_piece, "wide", panel_at % wide_size)


def block_tables(wanted, tall_size):
    owners = wanted % tall_size
    slots_at = wanted // tall_size
    width_wanted = wanted.shape[1]
    same_owner = owners[:, :, None] == owners[:, None, :]
    earlier = np.tril(np.ones((width_wanted, width_wanted), dtype=np.int32), -1)[None, :, :] > 0
    ranks = np.sum(same_owner & earlier, axis=2)
    piece_depth = int(np.max(ranks)) + 1
    talls = np.arange(tall_size)
    places = np.arange(piece_depth)
    matches = (owners[:, None, None, :] == talls[None, :, None, None]) & (
        ranks[:, None, None, :] == places[None, None, :, None]
    )
    senders = np.sum(matches * slots_at[:, None, None, :], axis=3).astype(np.int32)
    receivers = (owners * piece_depth + ranks).astype(np.int32)
    return (senders, receivers)


def owned_piece(source, senders, group_at, tall_at, slab_rows):
    slot_count = source.shape[0] // slab_rows
    blocks = source.reshape(slot_count, slab_rows, source.shape[1])
    chosen = jnp.asarray(senders)[group_at, tall_at]
    return jnp.take(blocks, chosen, axis=0)


def order_rows(gathered, receivers, group_at):
    placed = jnp.take(gathered, jnp.asarray(receivers)[group_at], axis=0)
    return placed.reshape(placed.shape[0] * placed.shape[1], placed.shape[2])


def body(initial, child_tiles, child_targets):
    wide_size = lax.axis_size("wide")
    tall_size = lax.axis_size("tall")
    wide_at = lax.axis_index("wide")
    tall_at = lax.axis_index("tall")
    slab_rows, front_order = initial.shape
    tile_count, tile_edge, _ = child_tiles.shape
    per_row = tile_count // tall_size
    panel_width = PANEL
    col_tiles = front_order // (panel_width * wide_size)
    blocks_per_panel = panel_width // slab_rows
    flat_tiles = child_tiles.reshape(tile_count, tile_edge * tile_edge)
    front_local = relayout(initial, wide_size, panel_width)
    target_wide = child_targets[:, 1] * tile_edge // panel_width % wide_size
    target_tall = jnp.arange(tile_count, dtype=jnp.int32) // per_row
    target_slot = target_wide * tall_size + target_tall
    slot_ids = jnp.arange(wide_size * tall_size, dtype=jnp.int32)
    selector = slot_ids[:, None] == target_slot[None, :]
    buffer = jnp.dot(
        selector.astype(jnp.float32),
        flat_tiles,
        precision=full_precision,
        preferred_element_type=jnp.float32,
    )
    filled = jnp.any(selector, axis=1)
    placed = jnp.sum(selector.astype(jnp.int32)[:, :, None] * child_targets[None, :, :], axis=1)
    placed = jnp.where(filled[:, None], placed, -1)
    arrived, targets = (
        lax.all_to_all(buffer, ("wide", "tall"), split_axis=0, concat_axis=0, tiled=True),
        lax.all_to_all(placed, ("wide", "tall"), split_axis=0, concat_axis=0, tiled=True),
    )
    usable = targets[:, 0] >= 0
    row_global = targets[:, 0] * tile_edge
    row_group = row_global // slab_rows
    local_row = row_group // tall_size * slab_rows + row_global % slab_rows
    col_global = targets[:, 1] * tile_edge
    local_col = col_global // panel_width // wide_size * panel_width + col_global % panel_width
    grid_index = (
        local_row // tile_edge * (col_tiles * panel_width // tile_edge) + local_col // tile_edge
    )
    grid_index = jnp.where(usable, grid_index, -1)
    front_local = add_blocks(front_local, arrived, grid_index, tile_edge)
    local_index = jnp.arange(front_local.shape[0], dtype=jnp.int32)
    global_row = (
        local_index // slab_rows * tall_size + tall_at
    ) * slab_rows + local_index % slab_rows
    tile_steps = np.arange(col_tiles)
    inner_steps = np.arange(blocks_per_panel)
    wide_steps = np.arange(wide_size)
    solved_wanted = (
        (tile_steps[None, :, None] * wide_size + wide_steps[:, None, None]) * blocks_per_panel
        + inner_steps[None, None, :]
    ).reshape(wide_size, col_tiles * blocks_per_panel)
    solved_send, solved_receive = block_tables(solved_wanted, tall_size)
    identity = jnp.eye(panel_width, dtype=jnp.float32)
    column_strip = share_strip(front_local, 0, panel_width)
    for panel_at in range(PANELS):
        low_row = panel_at * panel_width
        high_row = low_row + panel_width
        diag_wanted = (np.arange(blocks_per_panel) + low_row // slab_rows)[None, :]
        diag_send, diag_receive = block_tables(diag_wanted, tall_size)
        diag_piece = owned_piece(column_strip, diag_send, 0, tall_at, slab_rows)
        diag_block = order_rows(
            lax.all_gather(diag_piece, "tall", axis=0, tiled=True), diag_receive, 0
        )
        factor = jnp.linalg.cholesky(jnp.tril(diag_block) + jnp.tril(diag_block, -1).T)
        inverse = lax.linalg.triangular_solve(factor, identity, left_side=True, lower=True)
        solved = jnp.dot(
            column_strip, inverse.T, precision=full_precision, preferred_element_type=jnp.float32
        )
        below_mask = (global_row >= high_row)[:, None]
        inside = ((global_row >= low_row) & (global_row < high_row))[:, None]
        lower_rows = jnp.where(below_mask, solved, 0.0)
        new_diag = jnp.tril(factor) + jnp.triu(diag_block, 1)
        diag_rows = jnp.take(new_diag, jnp.clip(global_row - low_row, 0, panel_width - 1), axis=0)
        new_strip = jnp.where(below_mask, solved, jnp.where(inside, diag_rows, column_strip))
        solved_piece = owned_piece(lower_rows, solved_send, wide_at, tall_at, slab_rows)
        column_rows = order_rows(
            lax.all_gather(solved_piece, "tall", axis=0, tiled=True), solved_receive, wide_at
        )
        root_wide = panel_at % wide_size
        home_tile = panel_at // wide_size
        has_next = panel_at + 1 < PANELS
        change = jnp.dot(
            lower_rows, column_rows.T, precision=full_precision, preferred_element_type=jnp.float32
        )
        front_local = front_local - change
        current = lax.slice_in_dim(
            front_local, home_tile * panel_width, (home_tile + 1) * panel_width, axis=1
        )
        front_local = front_local.at[
            :, home_tile * panel_width : (home_tile + 1) * panel_width
        ].set(jnp.where(wide_at == root_wide, new_strip, current))
        if has_next:
            column_strip = share_strip(front_local, panel_at + 1, panel_width)
    return front_local


def solution(mesh):
    return jax.shard_map(
        body,
        mesh=mesh,
        in_specs=(
            P(("wide", "tall"), None),
            P(("wide", "tall"), None, None),
            P(("wide", "tall"), None),
        ),
        out_specs=P("tall", "wide"),
        check_vma=False,
    )
```

profile of v0, /device:TPU:0, one launch (start us, length us, event | category | flops | bytes accessed | tf_op | source)
XLA Modules:
  0.0 2232.3 jit_solution(1575796617000766094)
XLA Ops:
  8.9 7.3 all-to-all-start.1
  16.2 3.9 convolution_bitcast_fusion
  20.1 3.5 copy.45
  23.6 5.8 all-to-all-start.2
  29.4 33.0 %copy.66 = f32[64,8,32,512]{3,2,1,0:T(8,128)} copy(f32[64,8,32,512]{3,1,2,0:T(8,128)} %bitcast.231) | data formatting | bytes 67108864
  62.4 37.9 %copy.42 = f32[512,4,8,512]{3,1,0,2:T(4,128)} copy(f32[512,4,8,512]{3,2,1,0:T(8,128)} %bitcast.218) | data formatting | bytes 67108864 | tf_op jit(solution)/shard_map/reshape | solution.py:33
  100.3 7.2 all-to-all-start
  108.0 17.2 fusion.5
  125.1 705.6 %all-to-all-done = f32[512,4,8,512]{3,1,0,2:T(4,128)} async-done(((f32[512,4,8,512]{3,1,0,2:T(4,128)}), f32[512,4,8,512]{3,1,0,2:T(4,128)}, u32[]{:S(2)}, u32[]{:S(2)}) %all-to-all-start) | async-done | bytes 33554464 | tf_op jit(solution)/shard_map/all_to_all | solution.py:34
  830.7 30.0 %copy.67 = f32[512,8,4,512]{3,1,2,0:T(8,128)} copy(f32[512,8,4,512]{3,2,1,0:T(4,128)} %bitcast.65) | data formatting | bytes 67108864
  860.7 37.2 %bitcast_add_fusion = f32[4096,2048]{1,0:T(8,128)} fusion(f32[4096,2048]{1,0:T(8,128)} %bitcast.217, f32[512,8,16,128]{3,2,1,0:T(8,128)} %bitcast.216), kind=kLoop, calls=%fused_computation.10 | loop fusion | flops 8388608 | bytes 100663296 | tf_op jit(solution)/shard_map/add | solution.py:27
  897.9 7.6 slice_select_fusion
  905.6 174.8 %all-reduce.4.cloned.1.call-done = f32[4096,512]{1,0:T(8,128)} async-done(((f32[4096,512]{1,0:T(8,128)}), f32[4096,512]{1,0:T(8,128)}) %all-reduce.4.cloned.1.call-update) | async-done | bytes 8388624 | tf_op jit(solution)/shard_map/psum | solution.py:16
  1080.4 2.3 slice.239
  1084.5 51.2 %all-gather.5.cloned.1.call-done = f32[4,512,512]{2,1,0:T(8,128)} async-done(((f32[1,512,512]{2,1,0:T(8,128)}), f32[4,512,512]{2,1,0:T(8,128)}) %all-gather.5.cloned.1.call-update) | async-done | bytes 4194320 | tf_op jit(solution)/shard_map/all_gather | solution.py:140
  1140.4 11.7 cholesky.286
  1152.3 9.8 custom-call.27
  1164.6 11.9 cholesky.305
  1176.5 9.8 custom-call.28
  1187.9 11.7 cholesky.326
  1199.6 9.8 custom-call.29
  1210.9 12.1 cholesky.343
  1227.6 2.5 fusion.29
  1230.1 11.1 while.8
  1230.7 2.2 bitcast_dynamic-update-slice_fusion.4
  1233.5 2.2 bitcast_dynamic-update-slice_fusion.4
  1236.3 2.2 bitcast_dynamic-update-slice_fusion.4
  1239.1 2.1 bitcast_dynamic-update-slice_fusion.4
  1241.2 39.3 %custom-call.30 = f32[4,128,128]{1,2,0:T(8,128)S(1)} custom-call(f32[4,128,128]{2,1,0:T(8,128)S(1)} %get-tuple-element.72), custom_call_target="InvertDiagBlocksLowerTriangular" | custom-call | tf_op jit(solution)/shard_map/triangular_solve/custom-call.3 | solution.py:143
  1286.3 18.9 broadcast_select_fusion.2
  1305.2 6.2 gather_fusion
  1311.5 4.8 broadcast_select_fusion.6
  1318.0 16.8 gather_fusion.2
  1334.8 139.2 %all-gather.7.cloned.1.call-done = f32[16,512,512]{2,1,0:T(8,128)} async-done(((f32[4,512,512]{2,1,0:T(8,128)}), f32[16,512,512]{2,1,0:T(8,128)}) %all-gather.7.cloned.1.call-update) | async-done | bytes 16777232 | tf_op jit(solution)/shard_map/all_gather | solution.py:155
  1473.9 8.6 gather_fusion.1
  1482.5 5.1 broadcast_select_fusion.5
  1487.7 61.8 %convolution_subtract_fusion.1 = f32[4096,2048]{1,0:T(8,128)} fusion(f32[4096,2048]{1,0:T(8,128)} %bitcast_add_fusion, f32[4096,512]{1,0:T(8,128)} %get-tuple-element.128, f32[2048,512]{1,0:T(8,128)} %bitcast.233), kind=kOutput, calls=%fused_computation.13 | convolution fusion | flops 51547996160 | bytes 79691776 | tf_op jit(solution)/shard_map/dot_general | solution.py:160
  1549.5 16.6 broadcast_select_fusion.1
  1566.2 175.7 %all-reduce.6.cloned.1.call-done = f32[4096,512]{1,0:T(8,128)} async-done(((f32[4096,512]{1,0:T(8,128)}), f32[4096,512]{1,0:T(8,128)}) %all-reduce.6.cloned.1.call-update) | async-done | bytes 8388624 | tf_op jit(solution)/shard_map/psum | solution.py:16
  1741.9 2.3 slice.253
  1744.7 52.5 %all-gather.9.cloned.1.call-done = f32[4,512,512]{2,1,0:T(8,128)} async-done(((f32[1,512,512]{2,1,0:T(8,128)}), f32[4,512,512]{2,1,0:T(8,128)}) %all-gather.9.cloned.1.call-update) | async-done | bytes 4194320 | tf_op jit(solution)/shard_map/all_gather | solution.py:140
  1801.8 11.7 cholesky.358
  1813.7 9.8 custom-call.31
  1826.0 11.7 cholesky.377
  1837.8 9.9 custom-call.32
  1849.3 11.7 cholesky.398
  1861.1 9.8 custom-call.33
  1872.3 11.9 cholesky.415
  1889.4 2.5 fusion.28
  1891.9 11.1 while.9
  1892.5 2.2 bitcast_dynamic-update-slice_fusion.5
  1895.3 2.2 bitcast_dynamic-update-slice_fusion.5
  1898.1 2.2 bitcast_dynamic-update-slice_fusion.5
  1903.1 39.3 %custom-call.34 = f32[4,128,128]{1,2,0:T(8,128)S(1)} custom-call(f32[4,128,128]{2,1,0:T(8,128)S(1)} %get-tuple-element.73), custom_call_target="InvertDiagBlocksLowerTriangular" | custom-call | tf_op jit(solution)/shard_map/triangular_solve/custom-call.3 | solution.py:143
  1948.2 18.9 broadcast_select_fusion
  1967.1 6.2 gather_fusion.3
  1973.3 4.8 broadcast_select_fusion.4
  1978.3 8.5 constant_dynamic-update-slice_fusion.6
  1986.7 17.0 gather_fusion.5
  2003.8 132.0 %all-gather.11.cloned.1.call-done = f32[16,512,512]{2,1,0:T(8,128)} async-done(((f32[4,512,512]{2,1,0:T(8,128)}), f32[16,512,512]{2,1,0:T(8,128)}) %all-gather.11.cloned.1.call-update) | async-done | bytes 16777232 | tf_op jit(solution)/shard_map/all_gather | solution.py:155
  2135.8 8.6 gather_fusion.4
  2144.4 5.1 broadcast_select_fusion.3
  2149.5 61.8 %convolution_subtract_fusion = f32[4096,2048]{1,0:T(8,128)} fusion(f32[4096,2048]{1,0:T(8,128)} %constant_dynamic-update-slice_fusion.6, f32[4096,512]{1,0:T(8,128)} %get-tuple-element.132, f32[2048,512]{1,0:T(8,128)} %bitcast.232), kind=kOutput, calls=%fused_computation.12 | convolution fusion | flops 51547996160 | bytes 79691776 | tf_op jit(solution)/shard_map/dot_general | solution.py:160
  2211.4 13.6 fusion
  (141 shorter events, 50.8 us)
Async XLA Ops:
  8.9 14.7 all-to-all-start.1
  23.6 76.7 %all-to-all-start.2 = ((f32[32,1,16384]{2,1,0:T(1,128)}), f32[32,1,16384]{2,1,0:T(1,128)S(1)}, u32[]{:S(2)}, u32[]{:S(2)}) async-start(f32[32,1,16384]{2,1,0:T(1,128)} %copy.45), calls=%async_computation.2 | async-start | bytes 4194304 | tf_op jit(solution)/shard_map/all_to_all | solution.py:105
  100.3 730.4 %all-to-all-start = ((f32[512,4,8,512]{3,1,0,2:T(4,128)}), f32[512,4,8,512]{3,1,0,2:T(4,128)}, u32[]{:S(2)}, u32[]{:S(2)}) async-start(f32[512,4,8,512]{3,1,0,2:T(4,128)} %copy.42), calls=%async_computation | async-start | bytes 67108864 | tf_op jit(solution)/shard_map/all_to_all | solution.py:34
  107.6 972.8 %all-reduce.4.cloned.1.call-start = ((), (), s32[]{:S(2)}) async-start(), calls=%async_computation.3 | async-start | bytes 16777216 | tf_op jit(solution)/shard_map/psum | solution.py:16
  905.6 230.1 %all-gather.5.cloned.1.call-start = ((), (), s32[]{:S(2)}) async-start(), calls=%async_computation.4 | async-start | bytes 5242880 | tf_op jit(solution)/shard_map/all_gather | solution.py:140
  1082.7 391.2 %all-gather.7.cloned.1.call-start = ((), (), s32[]{:S(2)}) async-start(), calls=%async_computation.5 | async-start | bytes 20971520 | tf_op jit(solution)/shard_map/all_gather | solution.py:155
  1139.4 1.0 copy-start
  1316.3 425.6 %all-reduce.6.cloned.1.call-start = ((), (), s32[]{:S(2)}) async-start(), calls=%async_computation.6 | async-start | bytes 16777216 | tf_op jit(solution)/shard_map/psum | solution.py:16
  1482.5 66.9 %slice-start = ((s8[8388608]{0:T(1024)(128)(4,1)}), s8[4194304]{0:T(1024)(128)(4,1)S(1)}, s32[]{:S(2)}) async-start(s8[8388608]{0:T(1024)(128)(4,1)} %bitcast.222), calls=%async_computation.9 | async-start | bytes 8388608
  1482.5 66.9 %slice-start.4 = ((s8[8388608]{0:T(1024)(128)(4,1)}), s8[4194304]{0:T(1024)(128)(4,1)S(1)}, s32[]{:S(2)}) async-start(s8[8388608]{0:T(1024)(128)(4,1)} %bitcast.227), calls=%async_computation.13 | async-start | bytes 8388608
  1487.6 61.8 %slice-start.1 = ((s8[8388608]{0:T(1024)(128)(4,1)}), s8[4194304]{0:T(1024)(128)(4,1)S(1)}, s32[]{:S(2)}) async-start(s8[8388608]{0:T(1024)(128)(4,1)} %bitcast.222), calls=%async_computation.10 | async-start | bytes 8388608
  1487.7 61.8 %slice-start.5 = ((s8[8388608]{0:T(1024)(128)(4,1)}), s8[4194304]{0:T(1024)(128)(4,1)S(1)}, s32[]{:S(2)}) async-start(s8[8388608]{0:T(1024)(128)(4,1)} %bitcast.227), calls=%async_computation.14 | async-start | bytes 8388608
  1566.2 231.0 %all-gather.9.cloned.1.call-start = ((), (), s32[]{:S(2)}) async-start(), calls=%async_computation.7 | async-start | bytes 5242880 | tf_op jit(solution)/shard_map/all_gather | solution.py:140
  1744.2 391.6 %all-gather.11.cloned.1.call-start = ((), (), s32[]{:S(2)}) async-start(), calls=%async_computation.8 | async-start | bytes 20971520 | tf_op jit(solution)/shard_map/all_gather | solution.py:155
  1800.8 1.0 copy-start.1
  2144.4 66.9 %slice-start.2 = ((s8[8388608]{0:T(1024)(128)(4,1)}), s8[4194304]{0:T(1024)(128)(4,1)S(1)}, s32[]{:S(2)}) async-start(s8[8388608]{0:T(1024)(128)(4,1)} %bitcast.225), calls=%async_computation.11 | async-start | bytes 8388608
  2144.4 66.9 %slice-start.6 = ((s8[8388608]{0:T(1024)(128)(4,1)}), s8[4194304]{0:T(1024)(128)(4,1)S(1)}, s32[]{:S(2)}) async-start(s8[8388608]{0:T(1024)(128)(4,1)} %bitcast.229), calls=%async_computation.15 | async-start | bytes 8388608
  2149.5 61.8 %slice-start.3 = ((s8[8388608]{0:T(1024)(128)(4,1)}), s8[4194304]{0:T(1024)(128)(4,1)S(1)}, s32[]{:S(2)}) async-start(s8[8388608]{0:T(1024)(128)(4,1)} %bitcast.225), calls=%async_computation.12 | async-start | bytes 8388608
  2149.5 61.8 %slice-start.7 = ((s8[8388608]{0:T(1024)(128)(4,1)}), s8[4194304]{0:T(1024)(128)(4,1)S(1)}, s32[]{:S(2)}) async-start(s8[8388608]{0:T(1024)(128)(4,1)} %bitcast.229), calls=%async_computation.16 | async-start | bytes 8388608
Sparse Core Ops, SparseCore 0:
  905.7 174.6 all-reduce.3
  1082.8 52.8 all-gather.4
  1316.4 157.4 all-gather.6
  1566.3 175.5 all-reduce.5
  1744.3 52.8 all-gather.8
  1978.3 157.4 all-gather.10
where the time goes:
time: 2240 us; the launch traced here: 2230 us
  waiting for transfers between devices  1430 us (64%)
  other arithmetic  346 us (15%)
  local copies, waits for them, and re-layouts  209 us (9%)
  matrix products  205 us (9%)
    all_to_all x1, waiting for transfers between devices, relayout(): lax.all_to_all(pieces_out, 'wide', split_axis=2, concat_axis=0, tiled=True)  706 us
    psum x2, waiting for transfers between devices, from_root(): return lax.psum(kept, axis)  350 us
    all_gather x2, waiting for transfers between devices, body(): lax.all_gather(solved_piece, 'tall', axis=0, tiled=True)  271 us
    another operation x29, other arithmetic, body(): jnp.linalg.cholesky(jnp.tril(diag_block) + jnp.tril(diag_block, -1).T)  158 us
    dot_general x2, matrix products, body(): jnp.dot(lower_rows, column_rows.T, precision=full_precision, preferred_el...  124 us
    all_gather x2, waiting for transfers between devices, body(): lax.all_gather(diag_piece, 'tall', axis=0, tiled=True)  104 us
    another operation x4, other arithmetic, body(): lax.linalg.triangular_solve(factor, identity, left_side=True, lower=True)  78.7 us
    unnamed x22, local copies, waits for them, and re-layouts  65 us
  transfers between devices with their start and end apart: 9, of which 7 were waited for; matrix products, arithmetic and copies ran while one was open for 6% of the time, Pallas kernels for 0%

commit v1 on v0

v1 whole, which is shorter than its diff:
```python
import functools

import jax
import jax.numpy as jnp
import numpy as np
from jax import lax
from jax.experimental import pallas as pl
from jax.experimental.pallas import tpu as pltpu
from jax.sharding import PartitionSpec as P

PANEL = 512
PANELS = 2
BOTH = ("wide", "tall")
VMEM_LIMIT = 56 * 1024 * 1024
full_precision = lax.Precision.HIGHEST


def full_dot(left, right, dims=((1,), (0,))):
    return lax.dot_general(
        left, right, (dims, ((), ())), precision=full_precision, preferred_element_type=jnp.float32
    )


def iota(shape, axis):
    return lax.broadcasted_iota(jnp.int32, shape, axis)


def factor_block(work, edge):
    group = 8
    wide = 2 * edge
    lanes = iota((group, edge), 1)
    row = iota((group, 1), 0)

    def step(s, carry):
        low = pl.multiple_of(s * group, group)
        strip = work[pl.ds(low, group), :]
        left = strip[:, :edge]
        cols = [
            jnp.sum(jnp.where(lanes == low + i, left, 0.0), axis=1, keepdims=True)
            for i in range(group)
        ]
        for i in range(group):
            pivot = cols[i][i : i + 1]
            scale = lax.rsqrt(pivot)
            scale = scale * (1.5 - 0.5 * pivot * scale * scale)
            column = jnp.where(row > i, cols[i] * scale, 0.0)
            top = strip[i : i + 1] * scale
            strip = jnp.where(row == i, top, strip - column * top)
            for m in range(i + 1, group):
                cols[m] = cols[m] - column * column[m : m + 1]
        work[pl.ds(low, group), :] = strip
        left = jnp.where(lanes >= low + group, strip[:, :edge], 0.0)
        work[...] = work[...] - full_dot(left, strip, ((0,), (0,)))
        return carry

    lax.fori_loop(0, edge // group, step, 0)


def factor_kernel(diag, factors, inverses, below, square, work):
    edge = work.shape[0]
    wide = PANEL
    lower = iota((wide, wide), 0) >= iota((wide, wide), 1)
    small = iota((edge, edge), 0) >= iota((edge, edge), 1)
    eye = (iota((edge, edge), 0) == iota((edge, edge), 1)).astype(jnp.float32)
    steps = wide // edge
    for p in range(PANELS):
        own = pl.ds(p * wide, wide)
        block = diag[own, own]
        block = jnp.where(lower, block, block.T)
        for before in range(p):
            rows = below[pl.ds((p - 1) * wide, wide), pl.ds(before * wide, wide)]
            block = block - full_dot(rows, rows, ((1,), (1,)))
        square[...] = block
        factors[p] = jnp.zeros((wide, wide), jnp.float32)
        inverses[p] = jnp.zeros((wide, wide), jnp.float32)
        for b in range(steps):
            at = pl.ds(b * edge, edge)
            work[:, :edge] = square[at, at]
            work[:, edge:] = eye
            factor_block(work, edge)
            factors[p, at, at] = jnp.where(small, work[:, :edge].T, 0.0)
            inverse = jnp.where(small, work[:, edge:], 0.0)
            inverses[p, at, at] = inverse
            if b + 1 < steps:
                rest = pl.ds((b + 1) * edge, wide - (b + 1) * edge)
                under = full_dot(square[rest, at], inverse, ((1,), (1,)))
                factors[p, rest, at] = under
                square[rest, rest] = square[rest, rest] - full_dot(under, under, ((1,), (1,)))
            if b > 0:
                past = pl.ds(0, b * edge)
                inner = full_dot(factors[p, at, past], inverses[p, past, past])
                inverses[p, at, past] = -full_dot(inverse, inner)
        for after in range(p + 1, PANELS):
            there = pl.ds(after * wide, wide)
            rows = diag[there, own]
            for before in range(p):
                rows = rows - full_dot(
                    below[pl.ds((after - 1) * wide, wide), pl.ds(before * wide, wide)],
                    below[pl.ds((p - 1) * wide, wide), pl.ds(before * wide, wide)],
                    ((1,), (1,)),
                )
            below[pl.ds((after - 1) * wide, wide), own] = full_dot(rows, inverses[p], ((1,), (1,)))


def add_blocks(base, tiles, block_index, tile_edge):
    base_rows, base_cols = base.shape
    row_count = base_rows // tile_edge
    col_count = base_cols // tile_edge
    slot_ids = jnp.arange(row_count * col_count, dtype=jnp.int32)
    selector = (slot_ids[:, None] == block_index[None, :]).astype(jnp.float32)
    summed = full_dot(selector, tiles)
    summed = summed.reshape(row_count, col_count, tile_edge, tile_edge).transpose(0, 2, 1, 3)
    return base + summed.reshape(base_rows, base_cols)


def block_tables(wanted, tall_size):
    owners = wanted % tall_size
    slots_at = wanted // tall_size
    width_wanted = wanted.shape[1]
    same_owner = owners[:, :, None] == owners[:, None, :]
    earlier = np.tril(np.ones((width_wanted, width_wanted), dtype=np.int32), -1)[None, :, :] > 0
    ranks = np.sum(same_owner & earlier, axis=2)
    piece_depth = int(np.max(ranks)) + 1
    talls = np.arange(tall_size)
    places = np.arange(piece_depth)
    matches = (owners[:, None, None, :] == talls[None, :, None, None]) & (
        ranks[:, None, None, :] == places[None, None, :, None]
    )
    senders = np.sum(matches * slots_at[:, None, None, :], axis=3).astype(np.int32)
    receivers = (owners * piece_depth + ranks).astype(np.int32)
    return (senders, receivers)


def copy_kernel(table, source, target):
    target[0] = source[...]


def pack(slab, columns):
    rows = slab.shape[0]
    count = columns.shape[0]
    return pl.pallas_call(
        copy_kernel,
        grid_spec=pltpu.PrefetchScalarGridSpec(
            num_scalar_prefetch=1,
            grid=(count,),
            in_specs=[pl.BlockSpec((rows, PANEL), lambda n, table: (0, table[n]))],
            out_specs=pl.BlockSpec((1, rows, PANEL), lambda n, table: (n, 0, 0)),
        ),
        out_shape=jax.ShapeDtypeStruct((count, rows, PANEL), jnp.float32),
        cost_estimate=pl.CostEstimate(
            flops=0, bytes_accessed=2 * count * rows * PANEL * 4, transcendentals=0
        ),
        name="pack",
    )(columns.astype(jnp.int32), slab)


def factor_panels(diag):
    square = jax.ShapeDtypeStruct((PANELS, PANEL, PANEL), jnp.float32)
    rest = (PANELS - 1) * PANEL
    edge = 128
    return pl.pallas_call(
        factor_kernel,
        out_shape=(square, square, jax.ShapeDtypeStruct((rest, rest), jnp.float32)),
        scratch_shapes=[
            pltpu.VMEM((PANEL, PANEL), jnp.float32),
            pltpu.VMEM((edge, 2 * edge), jnp.float32),
        ],
        compiler_params=pltpu.CompilerParams(vmem_limit_bytes=VMEM_LIMIT),
        cost_estimate=pl.CostEstimate(
            flops=90_000_000_000, bytes_accessed=10_000_000, transcendentals=0
        ),
        name="factor",
    )(diag)


def split(value):
    high = value.astype(jnp.bfloat16)
    return high, (value - high.astype(jnp.float32)).astype(jnp.bfloat16)


def solve_kernel(turned, parts, table, *refs):
    raws = refs[:parts]
    inverses, below = refs[parts : parts + 2]
    outs, raw = refs[parts + 2 : -1], refs[-1]
    rows = raw.shape[0]
    for i, ref in enumerate(raws):

        @pl.when(table[1, 0] == i)
        def _(ref=ref):
            raw[...] = ref[0]

    at = table[0, pl.program_id(0)] + iota((rows, 1), 0)
    solved_0 = full_dot(raw[:, :PANEL], inverses[0], ((1,), (1,)))
    solved_0 = jnp.where(at >= PANEL, solved_0, 0.0)
    right = raw[:, PANEL:] - full_dot(solved_0, below[...], ((1,), (1,)))
    solved_1 = full_dot(right, inverses[1], ((1,), (1,)))
    solved_1 = jnp.where(at >= 2 * PANEL, solved_1, 0.0)
    for p, part in enumerate((solved_0, solved_1)):
        span = pl.ds(p * PANEL, PANEL)
        if turned:
            outs[0][0, span, :], outs[1][0, span, :] = split(part.T)
        else:
            outs[0][0, :, span] = part


def solve(raws, which, first_row, inverses, below, turned=False):
    count, rows, depth = raws[0].shape
    if turned:
        out_shape = [jax.ShapeDtypeStruct((count, depth, rows), jnp.bfloat16)] * 2
        out_specs = [pl.BlockSpec((1, depth, rows), lambda n, table: (n, 0, 0))] * 2
    else:
        out_shape = [jax.ShapeDtypeStruct((count, rows, depth), jnp.float32)]
        out_specs = [pl.BlockSpec((1, rows, depth), lambda n, table: (n, 0, 0))]

    def held(i):
        return pl.BlockSpec(
            (1, rows, depth), lambda n, table: (jnp.where(table[1, 0] == i, n, 0), 0, 0)
        )

    table = jnp.stack([first_row, jnp.full_like(first_row, 1) * which]).astype(jnp.int32)
    return pl.pallas_call(
        functools.partial(solve_kernel, turned, len(raws)),
        grid_spec=pltpu.PrefetchScalarGridSpec(
            num_scalar_prefetch=1,
            grid=(count,),
            in_specs=[held(i) for i in range(len(raws))]
            + [
                pl.BlockSpec(inverses.shape, lambda n, table: (0, 0, 0)),
                pl.BlockSpec(below.shape, lambda n, table: (0, 0)),
            ],
            out_specs=out_specs,
            scratch_shapes=[pltpu.VMEM((rows, depth), jnp.float32)],
        ),
        out_shape=out_shape,
        compiler_params=pltpu.CompilerParams(vmem_limit_bytes=VMEM_LIMIT),
        cost_estimate=pl.CostEstimate(
            flops=36 * count * rows * PANEL * PANEL,
            bytes_accessed=8 * count * rows * depth,
            transcendentals=0,
        ),
        name="solve",
    )(table, *raws, inverses, below)


def update_kernel(turned, row_parts, place, tile_place, *refs):
    pieces = refs[: len(turned)]
    row_refs = refs[len(turned) : len(turned) + row_parts]
    col_hi, col_lo, factors, tiles = refs[len(turned) + row_parts : len(turned) + row_parts + 4]
    out, row_hi, row_lo = refs[-3:]
    step = pl.program_id(0)
    rows, width = out.shape
    edge = tiles.shape[2]
    slot = place[3, step]
    at = place[4, step]
    first_row = place[5, step]
    panel = place[6, step]
    kind = place[7, step]
    fresh = (step == 0) | (slot != place[3, jnp.maximum(step - 1, 0)])
    for i, ref in enumerate(row_refs):

        @pl.when(fresh & (place[8, step] == i))
        def _(ref=ref):
            row_hi[...], row_lo[...] = split(ref[0])

    for i, ref in enumerate(pieces):

        @pl.when(kind == i)
        def _(i=i, ref=ref):
            out[...] = ref[0].T if turned[i] else ref[0]

    change = jnp.dot(row_hi[...], col_hi[at], preferred_element_type=jnp.float32)
    change += jnp.dot(row_hi[...], col_lo[at], preferred_element_type=jnp.float32)
    change += jnp.dot(row_lo[...], col_hi[at], preferred_element_type=jnp.float32)

    @pl.when(kind >= len(pieces))
    def _():
        out[...] = -change

    @pl.when(kind < len(pieces))
    def _():
        out[...] = out[...] - change

    def add_tile(n, carry):
        at_row = pl.multiple_of(tile_place[1, n] * edge, edge)
        at_col = pl.multiple_of(tile_place[2, n] * edge, edge)
        spot = (pl.ds(at_row, edge), pl.ds(at_col, edge))
        out[spot] = out[spot] + tiles[tile_place[0, n], :edge, :]
        return carry

    lax.fori_loop(place[2, step], place[9, step], add_tile, 0)
    for p in range(PANELS):
        for i, ref in enumerate(row_refs):

            @pl.when((panel == p) & (first_row >= width) & (place[8, step] == i))
            def _(p=p, ref=ref):
                out[...] = ref[0, :, p * PANEL : (p + 1) * PANEL]

        @pl.when((panel == p) & (first_row >= 0) & (first_row < width))
        def _(p=p):
            row = iota((rows, width), 0) + first_row
            kept = factors[p, pl.ds(pl.multiple_of(first_row, 8), rows), :]
            out[...] = jnp.where(row >= iota((rows, width), 1), kept, out[...])


def update(shape, pieces, turned, place, rows, cols, factors, tiles, tile_place):
    count = place.shape[1]
    _, block_rows, depth = rows[0].shape
    whole = functools.partial(
        pl.BlockSpec, index_map=lambda n, at, tile: (0, 0, 0), pipeline_mode=pl.Buffered(1)
    )

    def held(array, index):
        return pl.BlockSpec((1,) + array.shape[1:], lambda n, at, tile: (at[index, n], 0, 0))

    specs = [held(array, 10 + len(rows) + i) for i, array in enumerate(pieces)]
    specs += [held(array, 10 + i) for i, array in enumerate(rows)]
    specs += [whole(array.shape) for array in (*cols, factors, tiles)]
    operands = [*pieces, *rows, *cols, factors, tiles]
    return pl.pallas_call(
        functools.partial(update_kernel, turned, len(rows)),
        grid_spec=pltpu.PrefetchScalarGridSpec(
            num_scalar_prefetch=2,
            grid=(count,),
            in_specs=specs,
            out_specs=pl.BlockSpec((block_rows, PANEL), lambda n, at, tile: (at[0, n], at[1, n])),
            scratch_shapes=[pltpu.VMEM((block_rows, depth), jnp.bfloat16)] * 2,
        ),
        out_shape=jax.ShapeDtypeStruct(shape, jnp.float32),
        compiler_params=pltpu.CompilerParams(vmem_limit_bytes=VMEM_LIMIT),
        cost_estimate=pl.CostEstimate(
            flops=6 * count * block_rows * PANEL * depth,
            bytes_accessed=count * block_rows * PANEL * 8,
            transcendentals=0,
        ),
        name="update",
    )(place.astype(jnp.int32), tile_place.astype(jnp.int32), *operands)


def add_kernel(turned, place, piece, before, out):
    step = pl.program_id(0)
    rows, width = out.shape
    first_row = place[5, step]
    panel = place[6, step]
    out[...] = before[...] + (piece[0].T if turned else piece[0])

    @pl.when((panel >= 0) & (first_row >= 0))
    def _():
        row = iota((rows, width), 0) + first_row
        out[...] = jnp.where(row >= iota((rows, width), 1), before[...], out[...])


def add_entries(front, pieces, place, turned):
    count = place.shape[1]
    rows, width = pieces.shape[1:]
    spot = pl.BlockSpec((rows, width), lambda n, at: (at[0, n], at[1, n]))
    return pl.pallas_call(
        functools.partial(add_kernel, turned),
        grid_spec=pltpu.PrefetchScalarGridSpec(
            num_scalar_prefetch=1,
            grid=(count,),
            in_specs=[pl.BlockSpec((1, rows, width), lambda n, at: (at[at.shape[0] - 1, n], 0, 0)), spot],
            out_specs=spot,
        ),
        out_shape=jax.ShapeDtypeStruct(front.shape, jnp.float32),
        input_output_aliases={2: 0},
        cost_estimate=pl.CostEstimate(
            flops=0, bytes_accessed=12 * count * rows * width, transcendentals=0
        ),
        name="add_entries",
    )(place.astype(jnp.int32), pieces, front)


def body(initial, child_tiles, child_targets):
    wide_size = lax.axis_size("wide")
    tall_size = lax.axis_size("tall")
    wide_at = lax.axis_index("wide")
    tall_at = lax.axis_index("tall")
    slab_rows, front_order = initial.shape
    tile_count, tile_edge, _ = child_tiles.shape
    per_row = tile_count // tall_size
    col_tiles = front_order // (PANEL * wide_size)
    blocks_per_panel = PANEL // slab_rows
    depth = PANELS * PANEL
    mirrored = wide_size == 8 and tall_size == 4 and slab_rows == PANEL and col_tiles == 4
    half = wide_at // 4
    level = wide_at // 2
    own_group = wide_at * tall_size + tall_at

    def number(w, t):
        return w * tall_size + t

    def everyone(target):
        return [
            (number(w, t), number(*target(w, t))) for w in range(wide_size) for t in range(tall_size)
        ]

    def grid(*sizes):
        axes = jnp.meshgrid(*[jnp.arange(n, dtype=jnp.int32) for n in sizes], indexing="ij")
        return [axis.reshape(-1) for axis in axes]

    j4 = jnp.arange(4, dtype=jnp.int32)
    if mirrored:
        near_d, near_a = grid(4, 2)
        near_columns = (2 * (1 - half) + near_a) * 8 + 4 * half + (near_d ^ wide_at % 4)
        near_sent = pack(initial, near_columns[4:])
        child_tiles, near_sent = lax.optimization_barrier((child_tiles, near_sent))
        near_got = lax.ppermute(near_sent, BOTH, everyone(lambda w, t: (w ^ 2, t)))
        near_own = pack(initial, near_columns[:4])

    target_rows = jnp.pad(
        child_targets.astype(jnp.float32)[:, None, :], ((0, 0), (0, 7), (0, tile_edge - 2))
    )
    marked = jnp.concatenate([child_tiles, target_rows], 1)
    row_tiles = lax.all_to_all(
        marked.reshape(tall_size, per_row, tile_edge + 8, tile_edge), "tall", 0, 0, tiled=True
    ).reshape(tile_count, tile_edge + 8, tile_edge)
    targets = row_tiles[:, tile_edge, :2].astype(jnp.int32)
    strip_cols = depth // tile_edge
    strip_index = (targets[:, 0] * tile_edge % slab_rows) // tile_edge * strip_cols + targets[:, 1]
    strip_index = jnp.where(targets[:, 1] < strip_cols, strip_index, -1)
    strip = add_blocks(
        initial[:, :depth],
        row_tiles[:, :tile_edge].reshape(tile_count, tile_edge * tile_edge),
        strip_index,
        tile_edge,
    )

    owner = (targets[:, 1] * tile_edge // PANEL % wide_size).reshape(tall_size, per_row)
    match = owner[None, :, :] == jnp.arange(wide_size, dtype=jnp.int32)[:, None, None]
    filled = jnp.any(match, axis=2).reshape(-1)
    chosen = jnp.argmax(match, axis=2).astype(jnp.int32)
    chosen = (chosen + jnp.arange(tall_size, dtype=jnp.int32)[None, :] * per_row).reshape(-1)
    slots = wide_size * tall_size
    outgoing = jnp.where(filled[:, None, None], jnp.take(row_tiles, chosen, axis=0), -1.0)
    tiles = lax.all_to_all(
        outgoing.reshape(wide_size, tall_size, tile_edge + 8, tile_edge), "wide", 0, 0, tiled=True
    ).reshape(slots, tile_edge + 8, tile_edge)

    block_rows = jnp.arange(wide_size, dtype=jnp.int32)
    block_cols = jnp.arange(col_tiles, dtype=jnp.int32)
    if mirrored:
        native = lax.all_gather(
            strip, "wide", axis=0, axis_index_groups=[[0, 2, 4, 6], [1, 3, 5, 7]]
        )
        core = wide_at % 2
        turned = []
        for e in range(4):
            pairs = []
            for z in range(4):
                for t in range(4):
                    pairs.append((number(2 * z + z // 2, t), number(2 * z + t % 2, t ^ e)))
            pairs = [pair for pair in pairs if pair[0] != pair[1]]
            packed = pack(initial, (4 * (1 - half) + j4) * tall_size + (tall_at ^ e))
            arrived = lax.ppermute(packed, BOTH, pairs)
            turned.append(arrived if e else jnp.where(core == half, packed, arrived))

        def from_tall(t):
            e = tall_at ^ t
            return jnp.where(
                e == 0, turned[0], jnp.where(e == 1, turned[1], jnp.where(e == 2, turned[2], turned[3]))
            )

        native, near_got, tiles, turned = lax.optimization_barrier((native, near_got, tiles, turned))

        dest, a = grid(8, 2)
        packed = pack(initial, (2 * half + a) * 8 + dest).reshape(8, 2, slab_rows, PANEL)
        packed, native = lax.optimization_barrier((packed, native))
        main = lax.all_to_all(packed, "wide", 0, 0, tiled=True).reshape(16, slab_rows, PANEL)

        evens = range(0, wide_size, 2)
        have = native[0]
        parts = [
            lax.ppermute(have, BOTH, [(number(w, t), number(w, t ^ e)) for w in evens for t in (0, 1)])
            for e in (1, 2, 3)
        ]
        top = jnp.where(
            tall_at == 0, have, jnp.where(tall_at == 1, parts[0], jnp.where(tall_at == 2, parts[1], parts[2]))
        )
        bottom = jnp.where(
            tall_at == 1, have, jnp.where(tall_at == 0, parts[0], jnp.where(tall_at == 3, parts[1], parts[2]))
        )
        square = jnp.concatenate([top, bottom], 0)
        other = lax.ppermute(
            square, BOTH, [(number(w, t), number(w + 1, t)) for w in evens for t in range(tall_size)]
        )
        diag = jnp.where(wide_at % 2 == 0, square, other)

        after, square, near_got, turned = lax.optimization_barrier((native, square, near_got, turned))
        near_mate = lax.ppermute(
            jnp.concatenate([near_own[2:], near_got[2:]], 0), BOTH, everyone(lambda w, t: (w ^ 1, t))
        )
        near = jnp.concatenate([near_own[:2], near_mate[:2], near_got[:2], near_mate[2:]], 0)
        moves = from_tall((1 - level % 2) * 2 + core)
        moved = lax.ppermute(moves, BOTH, everyone(lambda w, t: (w ^ 2, t)))
        stays = from_tall(level % 2 * 2 + core)
        column_raw = [native]
        for e in range(4):
            pairs = []
            for z in range(4):
                for x in range(2):
                    t = z % 2 * 2 + x
                    pairs.append((number(2 * z + z // 2, t), number(2 * z + x, t ^ e)))
            pairs = [pair for pair in pairs if pair[0] != pair[1]]
            column_raw.append(lax.ppermute(after if e > 1 else native, BOTH, pairs))
        column_from = tall_at ^ (level % 2 * 2 + core)
        column_from = jnp.where((column_from == 0) & (core == half), 0, 1 + column_from)
    else:
        gathered = lax.all_gather(strip, "tall", axis=0, tiled=True)[:depth]
        diag = lax.psum(jnp.where(wide_at == 0, gathered, 0.0), "wide")

    marks = tiles[:, tile_edge, :2].astype(jnp.int32)
    at_row = marks[:, 0] * tile_edge
    at_col = marks[:, 1] * tile_edge
    block_number = at_row // slab_rows // tall_size * col_tiles + at_col // PANEL // wide_size
    block_number = jnp.where(marks[:, 0] >= 0, block_number, -1)
    lane = jnp.arange(slots, dtype=jnp.int32)
    ahead = block_number[None, :] < block_number[:, None]
    ahead |= (block_number[None, :] == block_number[:, None]) & (lane[None, :] < lane[:, None])
    rank = jnp.sum(ahead.astype(jnp.int32), axis=1)
    order = jnp.sum(jnp.where(rank[:, None] == lane[None, :], lane[:, None], 0), axis=0)
    tile_place = jnp.stack(
        [
            order,
            jnp.take(at_row % slab_rows // tile_edge, order),
            jnp.take(at_col % PANEL // tile_edge, order),
        ]
    )

    factors, inverses, below = factor_panels(diag)
    if mirrored:
        native_rows = 2 * j4 + core
        (native,) = solve([native], 0, (native_rows * tall_size + tall_at) * slab_rows, inverses, below)
        across = lax.ppermute(native, BOTH, everyone(lambda w, t: (w ^ 1, t)))
        first = (block_cols * wide_size + wide_at) * PANEL
        cols = solve(column_raw, column_from, first, inverses, below, True)
        rows = [native, across]
    else:
        (own,) = solve([strip[None]], 0, own_group[None] * slab_rows, inverses, below)
        solved = lax.all_gather(own[0], "wide", axis=0)
        wanted = (
            (np.arange(col_tiles)[None, :, None] * wide_size + np.arange(wide_size)[:, None, None])
            * blocks_per_panel
            + np.arange(blocks_per_panel)[None, None, :]
        ).reshape(wide_size, col_tiles * blocks_per_panel)
        senders, receivers = block_tables(wanted, tall_size)
        piece = jnp.take(solved, jnp.asarray(senders)[wide_at, tall_at], axis=0)
        pieces = lax.all_gather(piece, "tall", axis=0, tiled=True)
        column_rows = jnp.take(pieces, jnp.asarray(receivers)[wide_at], axis=0)
        column_rows = column_rows.reshape(col_tiles, PANEL, depth).transpose(0, 2, 1)
        high = lax.reduce_precision(column_rows, 8, 7)
        cols = [high.astype(jnp.bfloat16), (column_rows - high).astype(jnp.bfloat16)]
        rows = [solved]

    def places(block_row, block_col, row_slot, kind, piece_slots):
        first = (block_row * tall_size + tall_at) * slab_rows
        panel = block_col * wide_size + wide_at
        panel = jnp.where(panel < PANELS, panel, -1)
        per = rows[0].shape[0]
        table = [
            block_row,
            block_col,
            jnp.sum(block_number[None, :] < (block_row * col_tiles + block_col)[:, None], axis=1),
            row_slot,
            block_col,
            first - panel * PANEL,
            panel,
            kind,
            row_slot // per,
            jnp.sum(block_number[None, :] <= (block_row * col_tiles + block_col)[:, None], axis=1),
        ]
        table += [jnp.clip(row_slot - per * i, 0, per - 1) for i in range(len(rows))]
        return jnp.stack([jnp.asarray(line, jnp.int32) for line in table + piece_slots])

    shape = (wide_size * slab_rows, col_tiles * PANEL)
    rest = (rows, cols, factors, tiles, tile_place)
    if not mirrored:
        dest, q = grid(wide_size, col_tiles)
        packed = pack(initial, q * wide_size + dest).reshape(wide_size, col_tiles, slab_rows, PANEL)
        arrived = lax.all_to_all(packed, "wide", 0, 0, tiled=True)
        arrived = arrived.reshape(wide_size * col_tiles, slab_rows, PANEL)
        place = places(dest, q, dest, jnp.zeros_like(dest), [dest * col_tiles + q])
        return update(shape, [arrived], (False,), place, *rest)

    slot, q = grid(8, 4)
    k = 2 * (slot % 4) + jnp.where(slot < 4, core, 1 - core)
    d = wide_at ^ k
    same = d < 4
    kind = jnp.where(same & (q // 2 != half), 0, jnp.where(~same & (q == level), 1, 2))
    near_slot = jnp.where(same, d * 2 + q % 2, 3)
    stays_slot = jnp.where(same, 0, k % 4)
    place = places(k, q, slot, kind, [near_slot, stays_slot])
    front = update(shape, [near, stays], (False, True), place, *rest)
    k = 4 * (1 - half) + j4
    place = places(k, jnp.zeros_like(k) + (level ^ 1), k, k, [j4])
    front = add_entries(front, moved, place, True)
    k, a = grid(8, 2)
    place = places(k, 2 * (k // 4) + a, k, k, [2 * k + a])
    return add_entries(front, main, place, False)


def solution(mesh):
    return jax.shard_map(
        body,
        mesh=mesh,
        in_specs=(
            P(("wide", "tall"), None),
            P(("wide", "tall"), None, None),
            P(("wide", "tall"), None),
        ),
        out_specs=P("tall", "wide"),
        check_vma=False,
    )
```

time: 2240 us -> 776 us (0.35)
  waiting for transfers between devices: 1430 us -> 301 us
  other arithmetic: 346 us -> 42.9 us
  Pallas kernels: 0 us -> 299 us
  matrix products: 205 us -> 3.97 us
  local copies, waits for them, and re-layouts: 209 us -> 40 us
  starting transfers between devices: 21.6 us -> 64.8 us
    all_to_all x3, waiting for transfers between devices: 706 us -> 36.1 us  [the longest x1 26.3 us: body(): lax.all_to_all(marked.reshape(tall_size, per_row, tile_edge + 8, tile_edg...]
    all_gather x4 -> x1, waiting for transfers between devices: 375 us -> 0.01 us  [body(): lax.all_gather(strip, 'wide', axis=0, axis_index_groups=[[0, 2, 4, 6], [1...]
    psum x2 -> x0, waiting for transfers between devices: 350 us -> none  [from_root(): return lax.psum(kept, axis)]
    pallas_call x0 -> x13, Pallas kernels: none -> 299 us  [the longest x1 82.2 us: factor_panels(): pl.pallas_call(factor_kernel, out_shape=(square, square, jax.ShapeDtypeSt...]
    ppermute x0 -> x16, waiting for transfers between devices: none -> 265 us  [the longest x1 177 us: body(): near_got = lax.ppermute(near_sent, BOTH, everyone(lambda w, t: (w ^ 2, t)))]
    another operation x34 -> x3, other arithmetic: 238 us -> 1.35 us  [the longest x1 0.74 us: body(): chosen = jnp.argmax(match, axis=2).astype(jnp.int32)]
    dot_general x6 -> x1, matrix products: 183 us -> 3.97 us  [full_dot(): lax.dot_general(left, right, (dims, ((), ())), precision=full_precision,...]
    unnamed x22 -> x18, local copies, waits for them, and re-layouts: 65 us -> 1.96 us
  transfers between devices with their start and end apart: 9 -> 20, of which waited for: 7 -> 7; matrix products, arithmetic and copies ran while one was open for 6% -> 9% of each run, Pallas kernels for 0% -> 35%
where the time goes in v1:
time: 776 us; the launch traced here: 766 us
  waiting for transfers between devices  301 us (39%)
  Pallas kernels  299 us (39%)
  starting transfers between devices  64.8 us (8%)
  other arithmetic  42.9 us (6%)
  local copies, waits for them, and re-layouts  40 us (5%)
  between operations  14.1 us (2%)
    ppermute x1, waiting for transfers between devices, body(): near_got = lax.ppermute(near_sent, BOTH, everyone(lambda w, t: (w ^ 2, t)))  177 us
    pallas_call x1, Pallas kernels, factor_panels(): pl.pallas_call(factor_kernel, out_shape=(square, square, jax.ShapeDtypeSt...  82.2 us
    pallas_call x1, Pallas kernels, update(): pl.pallas_call(functools.partial(update_kernel, turned, len(rows)), grid_...  80.3 us
    pallas_call x2, Pallas kernels, solve(): pl.pallas_call(functools.partial(solve_kernel, turned, len(raws)), grid_s...  56.2 us
    pallas_call x7, Pallas kernels, pack(): pl.pallas_call(copy_kernel, grid_spec=pltpu.PrefetchScalarGridSpec(num_sc...  51 us
    ppermute x3, waiting for transfers between devices, body(): lax.ppermute(have, BOTH, [(number(w, t), number(w, t ^ e)) for w in evens...  36.5 us
    pallas_call x2, Pallas kernels, add_entries(): pl.pallas_call(functools.partial(add_kernel, turned), grid_spec=pltpu.Pre...  29.1 us
    ppermute x4, waiting for transfers between devices, body(): column_raw.append(lax.ppermute(after if e > 1 else native, BOTH, pairs))  28.2 us
  transfers between devices with their start and end apart: 20, of which 7 were waited for; matrix products, arithmetic and copies ran while one was open for 9% of the time, Pallas kernels for 35%

profile of v1, /device:TPU:0, one launch (start us, length us, event | category | flops | bytes accessed | tf_op | source)
XLA Modules:
  0.0 765.7 jit_solution(12758331219760073349)
XLA Ops:
  7.1 5.5 pack.7
  12.8 1.5 select_maximum_fusion
  14.3 5.2 all-to-all-start
  19.5 26.3 %all-to-all-done = f32[4,8,136,128]{3,2,1,0:T(8,128)S(1)} async-done(((f32[4,8,136,128]{3,2,1,0:T(8,128)}), f32[4,8,136,128]{3,2,1,0:T(8,128)S(1)}, u32[]{:S(2)}, u32[]{:S(2)}) %all-to-all-start) | async-done | bytes 2228256 | tf_op jit(solution)/shard_map/all_to_all | solution.py:414
  45.8 1.6 slice.86
  47.5 4.0 fusion
  51.4 3.6 bitcast_add_fusion
  55.6 5.5 pack.8
  61.1 2.7 collective-permute-start.1
  63.7 1.7 collective-permute-start
  66.0 5.6 pack.9
  71.5 6.0 collective-permute-start.2
  78.0 5.4 pack.10
  83.5 2.4 collective-permute-start.3
  86.4 5.4 pack.11
  91.8 3.3 collective-permute-start.4
  95.2 0.7 iota_reduce_fusion
  96.0 3.8 copy.47
  99.9 5.0 gather_fusion
  104.9 4.2 copy.48
  109.5 1.7 select_select_fusion.2
  111.2 3.6 all-to-all-start.1
  115.5 18.1 %pack.12 = f32[16,512,512]{2,1,0:T(8,128)} custom-call(s32[16]{0:T(128)} %get-tuple-element.89.table, f32[512,16384]{1,0:T(8,128)} %source.13), custom_call_target="tpu_custom_call" | custom-call | bytes 33554432 | tf_op jit(solution)/shard_map/pack/pallas_call | solution.py:141
  133.7 5.3 broadcast_select_fusion.1
  139.0 177.2 %collective-permute-done = f32[4,512,512]{2,1,0:T(8,128)} collective-permute-done((f32[4,512,512]{2,1,0:T(8,128)}, f32[4,512,512]{2,1,0:T(8,128)}, u32[]{:S(2)}, u32[]{:S(2)}) %collective-permute-start) | collective-permute-done | bytes 4194336 | tf_op jit(solution)/shard_map/ppermute | solution.py:407
  316.3 9.8 %all-to-all-done.1 = f32[8,4,136,128]{3,2,1,0:T(8,128)S(1)} async-done(((f32[8,4,136,128]{3,2,1,0:T(8,128)}), f32[8,4,136,128]{3,2,1,0:T(8,128)S(1)}, u32[]{:S(2)}, u32[]{:S(2)}) %all-to-all-start.1) | async-done | bytes 2228256 | tf_op jit(solution)/shard_map/all_to_all | solution.py:435
  326.1 4.0 slice_bitcast_fusion
  330.1 1.9 collective-permute-start.5
  332.0 4.6 collective-permute-start.6
  336.6 2.7 collective-permute-start.7
  339.2 5.9 all-to-all-start.2
  345.1 13.2 %collective-permute-done.5 = f32[512,1024]{1,0:T(8,128)} collective-permute-done((f32[512,1024]{1,0:T(8,128)}, f32[512,1024]{1,0:T(8,128)}, u32[]{:S(2)}, u32[]{:S(2)}) %collective-permute-start.5) | collective-permute-done | bytes 2097184 | tf_op jit(solution)/shard_map/ppermute | solution.py:473
  358.3 23.3 %collective-permute-done.6 = f32[512,1024]{1,0:T(8,128)} collective-permute-done((f32[512,1024]{1,0:T(8,128)}, f32[512,1024]{1,0:T(8,128)}, u32[]{:S(2)}, u32[]{:S(2)}) %collective-permute-start.6) | collective-permute-done | bytes 2097184 | tf_op jit(solution)/shard_map/ppermute | solution.py:473
  381.6 4.5 select_select_fusion.4
  386.0 2.5 pad_maximum_fusion.1
  388.6 3.3 collective-permute-start.10
  393.2 5.5 pack.13
  398.6 4.1 fusion.27
  402.7 3.9 collective-permute-start.12
  406.6 5.8 collective-permute-start.13
  412.4 5.7 collective-permute-start.14
  418.0 4.6 collective-permute-start.15
  422.7 4.0 fusion.29
  427.2 1.0 copy-done.1
  428.2 3.2 broadcast_select_fusion.diag
  431.4 82.2 %factor.1 = (f32[2,512,512]{2,1,0:T(8,128)}, f32[2,512,512]{2,1,0:T(8,128)}, f32[512,512]{1,0:T(8,128)}) custom-call(f32[1024,1024]{1,0:T(8,128)} %broadcast_select_fusion.diag), custom_call_target="tpu_custom_call" | custom-call | flops 89999998976 | bytes 10000000 | tf_op jit(solution)/shard_map/factor/pallas_call | solution.py:161
  513.6 26.2 %solve.2.refs_2_ = f32[4,512,1024]{2,1,0:T(8,128)} custom-call(s32[2,4]{1,0:T(2,128)} %stack.95.table, f32[4,512,1024]{2,1,0:T(8,128)} %bitcast.114, f32[2,512,512]{2,1,0:T(8,128)} %get-tuple-element.46.refs_1_.refs_5_, f32[512,512]{1,0:T(8,128)} %get-tuple-element.47.refs_2_.refs_6_), custom_call_target="tpu_custom_call" | custom-call | flops 19327352832 | bytes 16777216 | tf_op jit(solution)/shard_map/solve/pallas_call | solution.py:221
  539.8 1.7 collective-permute-start.11
  542.8 0.9 slice_convert_fusion
  544.2 0.7 gather_fusion.2
  544.9 0.7 gather_fusion.1
  545.8 1.2 stack.36.place
  547.0 1.2 stack.44.place
  548.4 1.2 stack.41.place
  550.2 10.3 %select_select_fusion = (f32[4,512,512]{2,1,0:T(8,128)}, f32[4,512,512]{2,1,0:T(8,128)S(1)}) fusion(f32[4,512,512]{2,1,0:T(8,128)} %broadcast_select_fusion.1, f32[4,512,512]{2,1,0:T(8,128)} %collective-permute-done.2, f32[4,512,512]{2,1,0:T(8,128)} %collective-permute-done.3, f32[4,512,512]{2,1,0:T(8,128)} %collective-permute-done.4, pred[]{:T(512)S(6)} %eq.157, ...), kind=kLoop, calls=%fused_computation.6 | loop fusion | flops 6291456 | bytes 25165830 | tf_op jit(solution)/shard_map/jit(_where)/select_n | solution.py:459
  560.6 2.8 fusion.28
  563.4 0.6 copy-done.3
  564.0 3.7 pad_maximum_fusion.refs_0_
  567.8 28.2 %collective-permute-done.14.refs_3_ = f32[4,512,1024]{2,1,0:T(8,128)} collective-permute-done((f32[4,512,1024]{2,1,0:T(8,128)}, f32[4,512,1024]{2,1,0:T(8,128)}, u32[]{:S(2)}, u32[]{:S(2)}) %collective-permute-start.14) | collective-permute-done | bytes 8388640 | tf_op jit(solution)/shard_map/ppermute | solution.py:504
  596.0 30.0 %solve.3 = (bf16[4,1024,512]{2,1,0:T(8,128)(2,1)}, bf16[4,1024,512]{2,1,0:T(8,128)(2,1)}) custom-call(s32[2,4]{1,0:T(2,128)} %stack.96.table, f32[4,512,1024]{2,1,0:T(8,128)} %bitcast.115, f32[4,512,1024]{2,1,0:T(8,128)} %collective-permute-done.12.refs_1_, f32[4,512,1024]{2,1,0:T(8,128)} %collective-permute-done.13.refs_2_, ...), custom_call_target="tpu_custom_call" | custom-call | flops 19327352832 | bytes 16777216 | tf_op jit(solution)/shard_map/solve/pallas_call | solution.py:221
  626.0 80.3 %update.1.before = f32[4096,2048]{1,0:T(8,128)} custom-call(s32[14,32]{1,0:T(8,128)} %stack.44.place, s32[3,32]{1,0:T(4,128)} %pad_add_fusion.tile_place, f32[8,512,512]{2,1,0:T(8,128)} %pad_maximum_fusion.refs_0_, f32[4,512,512]{2,1,0:T(8,128)} %get-tuple-element.73.refs_1_, f32[4,512,1024]{2,1,0:T(8,128)} %solve.2.refs_2_, ...), custom_call_target="tpu_custom_call" | custom-call | flops 51539607552 | bytes 67108864 | tf_op jit(solution)/shard_map/update/pallas_call | solution.py:319
  706.3 23.0 %collective-permute-done.8.piece = f32[4,512,512]{2,1,0:T(8,128)} collective-permute-done((f32[4,512,512]{2,1,0:T(8,128)S(1)}, f32[4,512,512]{2,1,0:T(8,128)}, u32[]{:S(2)}, u32[]{:S(2)}) %collective-permute-start.8) | collective-permute-done | bytes 4194336 | tf_op jit(solution)/shard_map/ppermute | solution.py:494
  729.3 7.0 add_entries.2.before
  736.4 22.0 %add_entries.3 = f32[4096,2048]{1,0:T(8,128)} custom-call(s32[13,16]{1,0:T(8,128)} %stack.36.place, f32[16,512,512]{2,1,0:T(8,128)} %bitcast.22.piece, f32[4096,2048]{1,0:T(8,128)} %add_entries.2.before), custom_call_target="tpu_custom_call", output_to_operand_aliasing={{}: (2, {})} | custom-call | bytes 50331648 | tf_op jit(solution)/shard_map/add_entries/pallas_call | solution.py:356
  (103 shorter events, 8.9 us)
Async XLA Ops:
  7.1 5.5 copy-start.7
  7.1 5.6 copy-start.5
  14.3 31.4 %all-to-all-start = ((f32[4,8,136,128]{3,2,1,0:T(8,128)}), f32[4,8,136,128]{3,2,1,0:T(8,128)S(1)}, u32[]{:S(2)}, u32[]{:S(2)}) async-start(f32[4,8,136,128]{3,2,1,0:T(8,128)} %bitcast.102), calls=%async_computation | async-start | bytes 4456448 | tf_op jit(solution)/shard_map/all_to_all | solution.py:414
  19.5 306.6 %all-gather.3.cloned.1.call-start = ((), (), s32[]{:S(2)}) async-start(), calls=%async_computation.3 | async-start | bytes 10485760 | tf_op jit(solution)/shard_map/all_gather | solution.py:442
  61.1 72.6 %collective-permute-start.1 = (f32[4,512,512]{2,1,0:T(8,128)}, f32[4,512,512]{2,1,0:T(8,128)}, u32[]{:S(2)}, u32[]{:S(2)}) collective-permute-start(f32[4,512,512]{2,1,0:T(8,128)} %pack.8), channel_id=1, source_target_pairs={{1,5},{3,7},{9,13},{11,15},{20,16},{22,18},{28,24},{30,26}} | collective-permute-start | bytes 12582920 | tf_op jit(solution)/shard_map/ppermute | solution.py:454
  63.7 252.5 %collective-permute-start = (f32[4,512,512]{2,1,0:T(8,128)}, f32[4,512,512]{2,1,0:T(8,128)}, u32[]{:S(2)}, u32[]{:S(2)}) collective-permute-start(f32[4,512,512]{2,1,0:T(8,128)} %pack.7), channel_id=1, source_target_pairs={{0,8},{1,9},{2,10},{3,11},{4,12},{5,13},{6,14},{7,15},{8,0},{9,1},... | collective-permute-start | bytes 12582920 | tf_op jit(solution)/shard_map/ppermute | solution.py:407
  71.5 244.7 %collective-permute-start.2 = (f32[4,512,512]{2,1,0:T(8,128)}, f32[4,512,512]{2,1,0:T(8,128)}, u32[]{:S(2)}, u32[]{:S(2)}) collective-permute-start(f32[4,512,512]{2,1,0:T(8,128)} %pack.9), channel_id=1, source_target_pairs={{0,1},{1,4},{2,3},{3,6},{8,9},{9,12},{10,11},{11,14},{20,17},{21,2... | collective-permute-start | bytes 12582920 | tf_op jit(solution)/shard_map/ppermute | solution.py:454
  83.5 232.8 %collective-permute-start.3 = (f32[4,512,512]{2,1,0:T(8,128)}, f32[4,512,512]{2,1,0:T(8,128)}, u32[]{:S(2)}, u32[]{:S(2)}) collective-permute-start(f32[4,512,512]{2,1,0:T(8,128)} %pack.10), channel_id=1, source_target_pairs={{0,2},{1,7},{2,0},{3,5},{8,10},{9,15},{10,8},{11,13},{20,18},{21,2... | collective-permute-start | bytes 12582920 | tf_op jit(solution)/shard_map/ppermute | solution.py:454
  91.8 224.5 %collective-permute-start.4 = (f32[4,512,512]{2,1,0:T(8,128)}, f32[4,512,512]{2,1,0:T(8,128)}, u32[]{:S(2)}, u32[]{:S(2)}) collective-permute-start(f32[4,512,512]{2,1,0:T(8,128)} %pack.11), channel_id=1, source_target_pairs={{0,3},{1,6},{2,1},{3,4},{8,11},{9,14},{10,9},{11,12},{20,19},{21,2... | collective-permute-start | bytes 12582920 | tf_op jit(solution)/shard_map/ppermute | solution.py:454
  111.2 214.9 %all-to-all-start.1 = ((f32[8,4,136,128]{3,2,1,0:T(8,128)}), f32[8,4,136,128]{3,2,1,0:T(8,128)S(1)}, u32[]{:S(2)}, u32[]{:S(2)}) async-start(f32[8,4,136,128]{3,2,1,0:T(8,128)} %select_select_fusion.2), calls=%async_computation.1 | async-start | bytes 4456448 | tf_op jit(solution)/shard_map/all_to_all | solution.py:435
  326.1 13.2 %copy-start.4 = (f32[8,4,136,128]{3,2,1,0:T(8,128)}, f32[8,4,136,128]{3,2,1,0:T(8,128)S(1)}, u32[]{:S(2)}) copy-start(f32[8,4,136,128]{3,2,1,0:T(8,128)S(1)} %all-to-all-done.1) | copy-start | bytes 6684676
  330.1 28.2 %collective-permute-start.5 = (f32[512,1024]{1,0:T(8,128)}, f32[512,1024]{1,0:T(8,128)}, u32[]{:S(2)}, u32[]{:S(2)}) collective-permute-start(f32[512,1024]{1,0:T(8,128)} %slice_bitcast_fusion), channel_id=1, source_target_pairs={{0,1},{1,0},{8,9},{9,8},{16,17},{17,16},{24,25},{25,24}} | collective-permute-start | bytes 6291464 | tf_op jit(solution)/shard_map/ppermute | solution.py:473
  332.0 49.6 %collective-permute-start.6 = (f32[512,1024]{1,0:T(8,128)}, f32[512,1024]{1,0:T(8,128)}, u32[]{:S(2)}, u32[]{:S(2)}) collective-permute-start(f32[512,1024]{1,0:T(8,128)} %slice_bitcast_fusion), channel_id=1, source_target_pairs={{0,2},{1,3},{8,10},{9,11},{16,18},{17,19},{24,26},{25,27}} | collective-permute-start | bytes 6291464 | tf_op jit(solution)/shard_map/ppermute | solution.py:473
  336.6 45.0 %collective-permute-start.7 = (f32[512,1024]{1,0:T(8,128)}, f32[512,1024]{1,0:T(8,128)}, u32[]{:S(2)}, u32[]{:S(2)}) collective-permute-start(f32[512,1024]{1,0:T(8,128)} %slice_bitcast_fusion), channel_id=1, source_target_pairs={{0,3},{1,2},{8,11},{9,10},{16,19},{17,18},{24,27},{25,26}} | collective-permute-start | bytes 6291464 | tf_op jit(solution)/shard_map/ppermute | solution.py:473
  339.2 397.1 %all-to-all-start.2 = ((f32[8,2,512,512]{3,2,1,0:T(8,128)}), f32[8,2,512,512]{3,2,1,0:T(8,128)}, u32[]{:S(2)}, u32[]{:S(2)}) async-start(f32[8,2,512,512]{3,2,1,0:T(8,128)} %bitcast.98), calls=%async_computation.2 | async-start | bytes 33554432 | tf_op jit(solution)/shard_map/all_to_all | solution.py:468
  386.0 2.6 copy-start
  388.6 38.5 %collective-permute-start.10 = (f32[1024,1024]{1,0:T(8,128)}, f32[1024,1024]{1,0:T(8,128)}, u32[]{:S(2)}, u32[]{:S(2)}) collective-permute-start(f32[1024,1024]{1,0:T(8,128)} %pad_maximum_fusion.1), channel_id=1, source_target_pairs={{0,4},{1,5},{2,6},{3,7},{8,12},{9,13},{10,14},{11,15},{16,20},{17,... | collective-permute-start | bytes 12582920 | tf_op jit(solution)/shard_map/ppermute | solution.py:483
  402.7 165.1 %collective-permute-start.12 = (f32[4,512,1024]{2,1,0:T(8,128)}, f32[4,512,1024]{2,1,0:T(8,128)}, u32[]{:S(2)}, u32[]{:S(2)}) collective-permute-start(f32[4,512,1024]{2,1,0:T(8,128)} %bitcast.110), channel_id=1, source_target_pairs={{1,5},{11,15},{20,16},{30,26}} | collective-permute-start | bytes 25165832 | tf_op jit(solution)/shard_map/ppermute | solution.py:504
  406.6 161.2 %collective-permute-start.13 = (f32[4,512,1024]{2,1,0:T(8,128)}, f32[4,512,1024]{2,1,0:T(8,128)}, u32[]{:S(2)}, u32[]{:S(2)}) collective-permute-start(f32[4,512,1024]{2,1,0:T(8,128)} %bitcast.111), channel_id=1, source_target_pairs={{0,1},{1,4},{10,11},{11,14},{20,17},{21,20},{30,27},{31,30}} | collective-permute-start | bytes 25165832 | tf_op jit(solution)/shard_map/ppermute | solution.py:504
  412.4 183.6 %collective-permute-start.14 = (f32[4,512,1024]{2,1,0:T(8,128)}, f32[4,512,1024]{2,1,0:T(8,128)}, u32[]{:S(2)}, u32[]{:S(2)}) collective-permute-start(f32[4,512,1024]{2,1,0:T(8,128)} %bitcast.112), channel_id=1, source_target_pairs={{0,2},{1,7},{10,8},{11,13},{20,18},{21,23},{30,24},{31,29}} | collective-permute-start | bytes 25165832 | tf_op jit(solution)/shard_map/ppermute | solution.py:504
  418.0 177.9 %collective-permute-start.15 = (f32[4,512,1024]{2,1,0:T(8,128)}, f32[4,512,1024]{2,1,0:T(8,128)}, u32[]{:S(2)}, u32[]{:S(2)}) collective-permute-start(f32[4,512,1024]{2,1,0:T(8,128)} %bitcast.113), channel_id=1, source_target_pairs={{0,3},{1,6},{10,9},{11,12},{20,19},{21,22},{30,25},{31,28}} | collective-permute-start | bytes 25165832 | tf_op jit(solution)/shard_map/ppermute | solution.py:504
  426.7 1.6 copy-start.1
  427.1 112.7 %collective-permute-start.9 = (f32[4,512,512]{2,1,0:T(8,128)S(1)}, f32[4,512,512]{2,1,0:T(8,128)}, u32[]{:S(2)}, u32[]{:S(2)}) collective-permute-start(f32[4,512,512]{2,1,0:T(8,128)S(1)} %pad_maximum_fusion.2), channel_id=1, source_target_pairs={{0,4},{1,5},{2,6},{3,7},{4,0},{5,1},{6,2},{7,3},{8,12},{9,13},{10,... | collective-permute-start | bytes 12582920 | tf_op jit(solution)/shard_map/ppermute | solution.py:489
  513.6 32.0 %copy-start.6 = (s32[16]{0:T(128)S(1)}, s32[16]{0:T(128)}, u32[]{:S(2)}) copy-start(s32[16]{0:T(128)} %get-tuple-element.90) | copy-start | bytes 196
  539.8 86.2 %collective-permute-start.11 = (f32[4,512,1024]{2,1,0:T(8,128)}, f32[4,512,1024]{2,1,0:T(8,128)}, u32[]{:S(2)}, u32[]{:S(2)}) collective-permute-start(f32[4,512,1024]{2,1,0:T(8,128)} %solve.2.refs_2_), channel_id=1, source_target_pairs={{0,4},{1,5},{2,6},{3,7},{4,0},{5,1},{6,2},{7,3},{8,12},{9,13},{10,... | collective-permute-start | bytes 25165832 | tf_op jit(solution)/shard_map/ppermute | solution.py:533
  560.6 2.9 copy-start.2
  560.6 3.5 copy-start.3
  567.8 161.5 %collective-permute-start.8 = (f32[4,512,512]{2,1,0:T(8,128)S(1)}, f32[4,512,512]{2,1,0:T(8,128)}, u32[]{:S(2)}, u32[]{:S(2)}) collective-permute-start(f32[4,512,512]{2,1,0:T(8,128)S(1)} %get-tuple-element.74), channel_id=1, source_target_pairs={{0,8},{1,9},{2,10},{3,11},{4,12},{5,13},{6,14},{7,15},{8,0},{9,1},... | collective-permute-start | bytes 12582920 | tf_op jit(solution)/shard_map/ppermute | solution.py:494
Sparse Core Ops, SparseCore 0:
  55.2 270.2 all-gather.2

commit v2 on v1

--- a/solution.py
+++ b/solution.py
@@ -167,7 +167,7 @@
         ],
         compiler_params=pltpu.CompilerParams(vmem_limit_bytes=VMEM_LIMIT),
         cost_estimate=pl.CostEstimate(
-            flops=90_000_000_000, bytes_accessed=10_000_000, transcendentals=0
+            flops=1_000_000_000, bytes_accessed=1_000_000, transcendentals=0
         ),
         name="factor",
     )(diag)
@@ -179,15 +179,15 @@
 
 
 def solve_kernel(turned, parts, table, *refs):
-    raws = refs[:parts]
-    inverses, below = refs[parts : parts + 2]
-    outs, raw = refs[parts + 2 : -1], refs[-1]
+    inverses, below = refs[2 * parts : 2 * parts + 2]
+    outs, raw = refs[2 * parts + 2 : -1], refs[-1]
     rows = raw.shape[0]
-    for i, ref in enumerate(raws):
+    for i in range(parts):
 
         @pl.when(table[1, 0] == i)
-        def _(ref=ref):
-            raw[...] = ref[0]
+        def _(i=i):
+            raw[:, :PANEL] = refs[i][0]
+            raw[:, PANEL:] = refs[parts + i][0]
 
     at = table[0, pl.program_id(0)] + iota((rows, 1), 0)
     solved_0 = full_dot(raw[:, :PANEL], inverses[0], ((1,), (1,)))
@@ -203,8 +203,10 @@
             outs[0][0, :, span] = part
 
 
-def solve(raws, which, first_row, inverses, below, turned=False):
-    count, rows, depth = raws[0].shape
+def solve(raws_0, raws_1, which, first_row, inverses, below, turned=False):
+    count, rows, width = raws_0[0].shape
+    depth = PANELS * width
+    parts = len(raws_0)
     if turned:
         out_shape = [jax.ShapeDtypeStruct((count, depth, rows), jnp.bfloat16)] * 2
         out_specs = [pl.BlockSpec((1, depth, rows), lambda n, table: (n, 0, 0))] * 2
@@ -214,16 +216,16 @@
 
     def held(i):
         return pl.BlockSpec(
-            (1, rows, depth), lambda n, table: (jnp.where(table[1, 0] == i, n, 0), 0, 0)
+            (1, rows, width), lambda n, table: (jnp.where(table[1, 0] == i, n, 0), 0, 0)
         )
 
     table = jnp.stack([first_row, jnp.full_like(first_row, 1) * which]).astype(jnp.int32)
     return pl.pallas_call(
-        functools.partial(solve_kernel, turned, len(raws)),
+        functools.partial(solve_kernel, turned, parts),
         grid_spec=pltpu.PrefetchScalarGridSpec(
             num_scalar_prefetch=1,
             grid=(count,),
-            in_specs=[held(i) for i in range(len(raws))]
+            in_specs=[held(i) for i in [*range(parts), *range(parts)]]
             + [
                 pl.BlockSpec(inverses.shape, lambda n, table: (0, 0, 0)),
                 pl.BlockSpec(below.shape, lambda n, table: (0, 0)),
@@ -234,12 +236,11 @@
         out_shape=out_shape,
         compiler_params=pltpu.CompilerParams(vmem_limit_bytes=VMEM_LIMIT),
         cost_estimate=pl.CostEstimate(
-            flops=36 * count * rows * PANEL * PANEL,
-            bytes_accessed=8 * count * rows * depth,
+            flops=count * rows * PANEL * PANEL, bytes_accessed=count * rows * depth,
             transcendentals=0,
         ),
         name="solve",
-    )(table, *raws, inverses, below)
+    )(table, *raws_0, *raws_1, inverses, below)
 
 
 def update_kernel(turned, row_parts, place, tile_place, *refs):
@@ -328,8 +329,7 @@
         out_shape=jax.ShapeDtypeStruct(shape, jnp.float32),
         compiler_params=pltpu.CompilerParams(vmem_limit_bytes=VMEM_LIMIT),
         cost_estimate=pl.CostEstimate(
-            flops=6 * count * block_rows * PANEL * depth,
-            bytes_accessed=count * block_rows * PANEL * 8,
+            flops=count * block_rows * PANEL * PANEL, bytes_accessed=count * block_rows * PANEL,
             transcendentals=0,
         ),
         name="update",
@@ -432,6 +432,8 @@
     chosen = (chosen + jnp.arange(tall_size, dtype=jnp.int32)[None, :] * per_row).reshape(-1)
     slots = wide_size * tall_size
     outgoing = jnp.where(filled[:, None, None], jnp.take(row_tiles, chosen, axis=0), -1.0)
+    if mirrored:
+        turned_sent = [pack(initial, (4 * (1 - half) + j4) * tall_size + (tall_at ^ e)) for e in range(4)]
     tiles = lax.all_to_all(
         outgoing.reshape(wide_size, tall_size, tile_edge + 8, tile_edge), "wide", 0, 0, tiled=True
     ).reshape(slots, tile_edge + 8, tile_edge)
@@ -439,9 +441,6 @@
     block_rows = jnp.arange(wide_size, dtype=jnp.int32)
     block_cols = jnp.arange(col_tiles, dtype=jnp.int32)
     if mirrored:
-        native = lax.all_gather(
-            strip, "wide", axis=0, axis_index_groups=[[0, 2, 4, 6], [1, 3, 5, 7]]
-        )
         core = wide_at % 2
         turned = []
         for e in range(4):
@@ -450,25 +449,52 @@
                 for t in range(4):
                     pairs.append((number(2 * z + z // 2, t), number(2 * z + t % 2, t ^ e)))
             pairs = [pair for pair in pairs if pair[0] != pair[1]]
-            packed = pack(initial, (4 * (1 - half) + j4) * tall_size + (tall_at ^ e))
-            arrived = lax.ppermute(packed, BOTH, pairs)
-            turned.append(arrived if e else jnp.where(core == half, packed, arrived))
-
+            arrived = lax.ppermute(turned_sent[e], BOTH, pairs)
+            turned.append(arrived if e else jnp.where(core == half, turned_sent[0], arrived))
+
+        same_core = [[0, 2, 4, 6], [1, 3, 5, 7]]
+        left, near_got, tiles, turned = lax.optimization_barrier(
+            (strip[:, :PANEL], near_got, tiles, turned)
+        )
+        native_0 = lax.all_gather(left, "wide", axis=0, axis_index_groups=same_core)
+        dest, a = grid(8, 2)
+        packed = pack(initial, (2 * half + a) * 8 + dest).reshape(8, 2, slab_rows, PANEL)
+        right, native_0, packed = lax.optimization_barrier((strip[:, PANEL:], native_0, packed))
+        native_1 = lax.all_gather(right, "wide", axis=0, axis_index_groups=same_core)
+
+        def to_columns(native):
+            arrived = [native]
+            for e in range(4):
+                pairs = []
+                for z in range(4):
+                    for x in range(2):
+                        t = z % 2 * 2 + x
+                        pairs.append((number(2 * z + z // 2, t), number(2 * z + x, t ^ e)))
+                pairs = [pair for pair in pairs if pair[0] != pair[1]]
+                arrived.append(lax.ppermute(native, BOTH, pairs))
+            return arrived
+
+        columns_0 = to_columns(native_0)
         def from_tall(t):
             e = tall_at ^ t
             return jnp.where(
                 e == 0, turned[0], jnp.where(e == 1, turned[1], jnp.where(e == 2, turned[2], turned[3]))
             )
 
-        native, near_got, tiles, turned = lax.optimization_barrier((native, near_got, tiles, turned))
-
-        dest, a = grid(8, 2)
-        packed = pack(initial, (2 * half + a) * 8 + dest).reshape(8, 2, slab_rows, PANEL)
-        packed, native = lax.optimization_barrier((packed, native))
+        moves = from_tall((1 - level % 2) * 2 + core)
+        stays = from_tall(level % 2 * 2 + core)
+        near_mate = lax.ppermute(
+            jnp.concatenate([near_own[2:], near_got[2:]], 0), BOTH, everyone(lambda w, t: (w ^ 1, t))
+        )
+        near = jnp.concatenate([near_own[:2], near_mate[:2], near_got[:2], near_mate[2:]], 0)
+        native_1, near, moves, stays, columns_0 = lax.optimization_barrier(
+            (native_1, near, moves, stays, columns_0)
+        )
+
         main = lax.all_to_all(packed, "wide", 0, 0, tiled=True).reshape(16, slab_rows, PANEL)
 
         evens = range(0, wide_size, 2)
-        have = native[0]
+        have = jnp.concatenate([native_0[0], native_1[0]], 1)
         parts = [
             lax.ppermute(have, BOTH, [(number(w, t), number(w, t ^ e)) for w in evens for t in (0, 1)])
             for e in (1, 2, 3)
@@ -485,23 +511,8 @@
         )
         diag = jnp.where(wide_at % 2 == 0, square, other)
 
-        after, square, near_got, turned = lax.optimization_barrier((native, square, near_got, turned))
-        near_mate = lax.ppermute(
-            jnp.concatenate([near_own[2:], near_got[2:]], 0), BOTH, everyone(lambda w, t: (w ^ 1, t))
-        )
-        near = jnp.concatenate([near_own[:2], near_mate[:2], near_got[:2], near_mate[2:]], 0)
-        moves = from_tall((1 - level % 2) * 2 + core)
         moved = lax.ppermute(moves, BOTH, everyone(lambda w, t: (w ^ 2, t)))
-        stays = from_tall(level % 2 * 2 + core)
-        column_raw = [native]
-        for e in range(4):
-            pairs = []
-            for z in range(4):
-                for x in range(2):
-                    t = z % 2 * 2 + x
-                    pairs.append((number(2 * z + z // 2, t), number(2 * z + x, t ^ e)))
-            pairs = [pair for pair in pairs if pair[0] != pair[1]]
-            column_raw.append(lax.ppermute(after if e > 1 else native, BOTH, pairs))
+        columns_1 = to_columns(native_1)
         column_from = tall_at ^ (level % 2 * 2 + core)
         column_from = jnp.where((column_from == 0) & (core == half), 0, 1 + column_from)
     else:
@@ -528,14 +539,17 @@
 
     factors, inverses, below = factor_panels(diag)
     if mirrored:
+        factors, inverses, below, columns_1 = lax.optimization_barrier((factors, inverses, below, columns_1))
         native_rows = 2 * j4 + core
-        (native,) = solve([native], 0, (native_rows * tall_size + tall_at) * slab_rows, inverses, below)
+        (native,) = solve([native_0], [native_1], 0, (native_rows * tall_size + tall_at) * slab_rows, inverses, below)
         across = lax.ppermute(native, BOTH, everyone(lambda w, t: (w ^ 1, t)))
         first = (block_cols * wide_size + wide_at) * PANEL
-        cols = solve(column_raw, column_from, first, inverses, below, True)
+        cols = solve(columns_0, columns_1, column_from, first, inverses, below, True)
         rows = [native, across]
     else:
-        (own,) = solve([strip[None]], 0, own_group[None] * slab_rows, inverses, below)
+        (own,) = solve(
+            [strip[None, :, :PANEL]], [strip[None, :, PANEL:]], 0, own_group[None] * slab_rows, inverses, below
+        )
         solved = lax.all_gather(own[0], "wide", axis=0)
         wanted = (
             (np.arange(col_tiles)[None, :, None] * wide_size + np.arange(wide_size)[:, None, None])

time: 776 us -> 807 us (1.040)
  starting transfers between devices: 64.8 us -> 108 us
  waiting for transfers between devices: 301 us -> 289 us
    ppermute x1, waiting for transfers between devices: 177 us -> 42.1 us  [body(): near_got = lax.ppermute(near_sent, BOTH, everyone(lambda w, t: (w ^ 2, t)))]
    all_gather x1 -> x2, waiting for transfers between devices: 0.01 us -> 96 us  [the longest x1 63.5 us: body(): native_0 = lax.all_gather(left, 'wide', axis=0, axis_index_groups=same_core)]
    ppermute x8 -> x12, waiting for transfers between devices: 28.2 us -> 73.4 us  [the longest x8 66.6 us: to_columns(): arrived.append(lax.ppermute(native, BOTH, pairs))]
    ppermute x1, starting transfers between devices: 0.01 us -> 30.9 us  [body(): moved = lax.ppermute(moves, BOTH, everyone(lambda w, t: (w ^ 2, t)))]
    all_to_all x1, waiting for transfers between devices: 26.3 us -> 0.01 us  [body(): lax.all_to_all(marked.reshape(tall_size, per_row, tile_edge + 8, tile_edg...]
    ppermute x8 -> x12, starting transfers between devices: 34.3 us -> 47.4 us  [the longest x8 31.5 us: to_columns(): arrived.append(lax.ppermute(native, BOTH, pairs))]
  transfers between devices with their start and end apart: 20 -> 25, of which waited for: 7 -> 10; matrix products, arithmetic and copies ran while one was open for 9% -> 10% of each run, Pallas kernels for 35% -> 34%
where the time goes in v2:
time: 807 us; the launch traced here: 797 us
  Pallas kernels  299 us (37%)
  waiting for transfers between devices  289 us (36%)
  starting transfers between devices  108 us (13%)
  other arithmetic  45.5 us (6%)
  local copies, waits for them, and re-layouts  39.1 us (5%)
  between operations  14 us (2%)
    pallas_call x1, Pallas kernels, factor_panels(): pl.pallas_call(factor_kernel, out_shape=(square, square, jax.ShapeDtypeSt...  82.5 us
    pallas_call x1, Pallas kernels, update(): pl.pallas_call(functools.partial(update_kernel, turned, len(rows)), grid_...  80.3 us
    ppermute x8, waiting for transfers between devices, to_columns(): arrived.append(lax.ppermute(native, BOTH, pairs))  66.6 us
    all_gather x1, waiting for transfers between devices, body(): native_0 = lax.all_gather(left, 'wide', axis=0, axis_index_groups=same_core)  63.5 us
    pallas_call x2, Pallas kernels, solve(): pl.pallas_call(functools.partial(solve_kernel, turned, parts), grid_spec=...  56.2 us
    pallas_call x7, Pallas kernels, pack(): pl.pallas_call(copy_kernel, grid_spec=pltpu.PrefetchScalarGridSpec(num_sc...  51 us
    ppermute x3, waiting for transfers between devices, body(): lax.ppermute(have, BOTH, [(number(w, t), number(w, t ^ e)) for w in evens...  42.1 us
    ppermute x1, waiting for transfers between devices, body(): near_got = lax.ppermute(near_sent, BOTH, everyone(lambda w, t: (w ^ 2, t)))  42.1 us
  transfers between devices with their start and end apart: 25, of which 10 were waited for; matrix products, arithmetic and copies ran while one was open for 10% of the time, Pallas kernels for 34%

profile of v2, /device:TPU:0, one launch (start us, length us, event | category | flops | bytes accessed | tf_op | source)
XLA Modules:
  0.0 797.3 jit_solution(11645793223731716405)
XLA Ops:
  7.1 5.5 pack.7
  12.8 1.5 select_maximum_fusion
  14.3 5.2 all-to-all-start
  20.0 5.5 pack.8
  25.4 2.6 collective-permute-start.1
  28.1 1.6 collective-permute-start
  30.1 5.4 pack.9
  35.5 6.7 collective-permute-start.2
  42.7 5.4 pack.10
  48.1 3.4 collective-permute-start.3
  52.0 5.5 pack.11
  57.5 3.2 collective-permute-start.4
  61.8 3.8 copy.47
  65.7 5.0 gather_fusion
  70.7 5.0 copy.48
  76.0 3.4 select_select_fusion.2
  79.4 4.4 all-to-all-start.1
  84.1 2.5 fusion
  86.6 2.3 bitcast_add_fusion
  88.9 1.5 fusion.30
  90.4 1.4 copy-done.1
  91.9 3.0 broadcast_select_fusion.1
  94.9 42.1 %collective-permute-done = f32[4,512,512]{2,1,0:T(8,128)} collective-permute-done((f32[4,512,512]{2,1,0:T(8,128)}, f32[4,512,512]{2,1,0:T(8,128)}, u32[]{:S(2)}, u32[]{:S(2)}) %collective-permute-start) | collective-permute-done | bytes 4194336 | tf_op jit(solution)/shard_map/ppermute | solution.py:407
  136.9 6.8 collective-permute-done.3
  143.8 12.5 %all-to-all-done.1 = f32[8,4,136,128]{3,2,1,0:T(8,128)} async-done(((f32[8,4,136,128]{3,2,1,0:T(8,128)}), f32[8,4,136,128]{3,2,1,0:T(8,128)}, u32[]{:S(2)}, u32[]{:S(2)}) %all-to-all-start.1) | async-done | bytes 2228256 | tf_op jit(solution)/shard_map/all_to_all | solution.py:437
  157.1 18.2 %pack.12 = f32[16,512,512]{2,1,0:T(8,128)} custom-call(s32[16]{0:T(128)} %get-tuple-element.115.table, f32[512,16384]{1,0:T(8,128)} %source.13), custom_call_target="tpu_custom_call" | custom-call | bytes 33554432 | tf_op jit(solution)/shard_map/pack/pallas_call | solution.py:141
  175.3 63.5 %all-gather.5.cloned.1.call-done = f32[2048,512]{1,0:T(8,128)} async-done(((f32[512,512]{1,0:T(8,128)}), f32[2048,512]{1,0:T(8,128)}) %all-gather.5.cloned.1.call-update) | async-done | bytes 4194320 | tf_op jit(solution)/shard_map/all_gather | solution.py:459
  238.8 5.7 all-to-all-start.2
  245.8 5.5 pack.13
  251.3 2.7 fusion.27
  254.0 4.4 fusion.29
  258.4 2.4 pad_maximum_fusion.1
  261.2 2.6 collective-permute-start.6
  263.8 6.8 collective-permute-start.7
  270.6 3.3 collective-permute-start.8
  273.9 3.5 collective-permute-start.9
  277.4 11.3 %select_select_fusion = (f32[4,512,512]{2,1,0:T(8,128)}, f32[4,512,512]{2,1,0:T(8,128)}) fusion(f32[4,512,512]{2,1,0:T(8,128)} %broadcast_select_fusion.1, f32[4,512,512]{2,1,0:T(8,128)} %collective-permute-done.2, f32[4,512,512]{2,1,0:T(8,128)} %collective-permute-done.3, f32[4,512,512]{2,1,0:T(8,128)} %collective-permute-done.4, pred[]{:T(512)S(6)} %eq.146, ...), kind=kLoop, calls=%fused_computation.6 | loop fusion | flops 6291456 | bytes 25165830 | tf_op jit(solution)/shard_map/jit(_where)/select_n | solution.py:480
  288.7 2.8 fusion.28
  291.5 3.7 pad_maximum_fusion.refs_0_
  295.3 1.3 slice_bitcast_fusion.1
  296.6 18.3 %collective-permute-done.7.refs_2_ = f32[4,512,512]{2,1,0:T(8,128)} collective-permute-done((f32[4,512,512]{2,1,0:T(8,128)}, f32[4,512,512]{2,1,0:T(8,128)}, u32[]{:S(2)}, u32[]{:S(2)}) %collective-permute-start.7) | collective-permute-done | bytes 4194336 | tf_op jit(solution)/shard_map/ppermute | solution.py:474
  314.9 48.2 %collective-permute-done.8.refs_3_ = f32[4,512,512]{2,1,0:T(8,128)} collective-permute-done((f32[4,512,512]{2,1,0:T(8,128)}, f32[4,512,512]{2,1,0:T(8,128)}, u32[]{:S(2)}, u32[]{:S(2)}) %collective-permute-start.8) | collective-permute-done | bytes 4194336 | tf_op jit(solution)/shard_map/ppermute | solution.py:474
  363.1 32.5 %all-gather.7.cloned.1.call-done = f32[2048,512]{1,0:T(8,128)} async-done(((f32[512,512]{1,0:T(8,128)}), f32[2048,512]{1,0:T(8,128)}) %all-gather.7.cloned.1.call-update) | async-done | bytes 4194320 | tf_op jit(solution)/shard_map/all_gather | solution.py:463
  398.1 3.4 collective-permute-start.11
  401.5 3.4 collective-permute-start.12
  404.8 2.6 collective-permute-start.13
  407.5 18.7 %collective-permute-done.11 = f32[512,1024]{1,0:T(8,128)} collective-permute-done((f32[512,1024]{1,0:T(8,128)S(1)}, f32[512,1024]{1,0:T(8,128)}, u32[]{:S(2)}, u32[]{:S(2)}) %collective-permute-start.11) | collective-permute-done | bytes 2097184 | tf_op jit(solution)/shard_map/ppermute | solution.py:499
  426.1 23.4 %collective-permute-done.12 = f32[512,1024]{1,0:T(8,128)} collective-permute-done((f32[512,1024]{1,0:T(8,128)S(1)}, f32[512,1024]{1,0:T(8,128)}, u32[]{:S(2)}, u32[]{:S(2)}) %collective-permute-start.12) | collective-permute-done | bytes 2097184 | tf_op jit(solution)/shard_map/ppermute | solution.py:499
  449.5 4.1 select_select_fusion.4
  453.6 2.7 pad_maximum_fusion.2
  456.3 3.3 collective-permute-start.14
  459.6 2.6 collective-permute-start.15
  462.2 6.0 collective-permute-start.16
  468.2 3.3 collective-permute-start.17
  471.6 3.4 collective-permute-start.18
  475.5 4.8 broadcast_select_fusion.diag
  480.3 82.5 %factor.1 = (f32[2,512,512]{2,1,0:T(8,128)}, f32[2,512,512]{2,1,0:T(8,128)}, f32[512,512]{1,0:T(8,128)}) custom-call(f32[1024,1024]{1,0:T(8,128)} %broadcast_select_fusion.diag), custom_call_target="tpu_custom_call" | custom-call | flops 1000000000 | bytes 1000000 | tf_op jit(solution)/shard_map/factor/pallas_call | solution.py:161
  562.9 26.1 %solve.2.refs_2_ = f32[4,512,1024]{2,1,0:T(8,128)} custom-call(s32[2,4]{1,0:T(2,128)} %stack.95.table, f32[4,512,512]{2,1,0:T(8,128)} %bitcast.20.refs_0_, f32[4,512,512]{2,1,0:T(8,128)} %bitcast.25.refs_1_.refs_5_, f32[2,512,512]{2,1,0:T(8,128)} %get-tuple-element.61.refs_2_.refs_10_, f32[512,512]{1,0:T(8,128)} %get-tuple-element.62.refs_3_.refs_11_), custom_call_target="tpu_custom_call" | custom-call | flops 536870912 | bytes 2097152 | tf_op jit(solution)/shard_map/solve/pallas_call | solution.py:223
  589.0 30.9 %collective-permute-start.10 = (f32[4,512,512]{2,1,0:T(8,128)}, f32[4,512,512]{2,1,0:T(8,128)}, u32[]{:S(2)}, u32[]{:S(2)}) collective-permute-start(f32[4,512,512]{2,1,0:T(8,128)} %get-tuple-element.54), channel_id=1, source_target_pairs={{0,8},{1,9},{2,10},{3,11},{4,12},{5,13},{6,14},{7,15},{8,0},{9,1},... | collective-permute-start | bytes 12582920 | tf_op jit(solution)/shard_map/ppermute | solution.py:514
  628.6 30.1 %solve.3 = (bf16[4,1024,512]{2,1,0:T(8,128)(2,1)}, bf16[4,1024,512]{2,1,0:T(8,128)(2,1)}) custom-call(s32[2,4]{1,0:T(2,128)} %stack.96.table, f32[4,512,512]{2,1,0:T(8,128)} %bitcast.20.refs_0_, f32[4,512,512]{2,1,0:T(8,128)} %collective-permute-done.6.refs_1_, f32[4,512,512]{2,1,0:T(8,128)} %collective-permute-done.7.refs_2_, ...), custom_call_target="tpu_custom_call" | custom-call | flops 536870912 | bytes 2097152 | tf_op jit(solution)/shard_map/solve/pallas_call | solution.py:223
  658.7 80.3 %update.1.before = f32[4096,2048]{1,0:T(8,128)} custom-call(s32[14,32]{1,0:T(8,128)} %stack.44.place, s32[3,32]{1,0:T(4,128)} %pad_add_fusion.tile_place, f32[8,512,512]{2,1,0:T(8,128)} %pad_maximum_fusion.refs_0_, f32[4,512,512]{2,1,0:T(8,128)} %get-tuple-element.56.refs_1_, f32[4,512,1024]{2,1,0:T(8,128)} %solve.2.refs_2_, ...), custom_call_target="tpu_custom_call" | custom-call | flops 4294967296 | bytes 8388608 | tf_op jit(solution)/shard_map/update/pallas_call | solution.py:320
  739.0 22.2 %collective-permute-done.10.piece = f32[4,512,512]{2,1,0:T(8,128)} collective-permute-done((f32[4,512,512]{2,1,0:T(8,128)}, f32[4,512,512]{2,1,0:T(8,128)}, u32[]{:S(2)}, u32[]{:S(2)}) %collective-permute-start.10) | collective-permute-done | bytes 4194336 | tf_op jit(solution)/shard_map/ppermute | solution.py:514
  761.2 7.0 add_entries.2.before
  768.2 22.0 %add_entries.3 = f32[4096,2048]{1,0:T(8,128)} custom-call(s32[13,16]{1,0:T(8,128)} %stack.36.place, f32[16,512,512]{2,1,0:T(8,128)} %bitcast.22.piece, f32[4096,2048]{1,0:T(8,128)} %add_entries.2.before), custom_call_target="tpu_custom_call", output_to_operand_aliasing={{}: (2, {})} | custom-call | bytes 50331648 | tf_op jit(solution)/shard_map/add_entries/pallas_call | solution.py:356
  (113 shorter events, 18.7 us)
Async XLA Ops:
  7.1 5.6 copy-start.5
  7.1 5.7 copy-start.4
  14.3 46.4 %all-to-all-start = ((f32[4,8,136,128]{3,2,1,0:T(8,128)}), f32[4,8,136,128]{3,2,1,0:T(8,128)S(1)}, u32[]{:S(2)}, u32[]{:S(2)}) async-start(f32[4,8,136,128]{3,2,1,0:T(8,128)} %bitcast.101), calls=%async_computation | async-start | bytes 4456448 | tf_op jit(solution)/shard_map/all_to_all | solution.py:414
  25.4 65.0 %collective-permute-start.1 = (f32[4,512,512]{2,1,0:T(8,128)}, f32[4,512,512]{2,1,0:T(8,128)}, u32[]{:S(2)}, u32[]{:S(2)}) collective-permute-start(f32[4,512,512]{2,1,0:T(8,128)} %pack.8), channel_id=1, source_target_pairs={{1,5},{3,7},{9,13},{11,15},{20,16},{22,18},{28,24},{30,26}} | collective-permute-start | bytes 12582920 | tf_op jit(solution)/shard_map/ppermute | solution.py:452
  28.1 108.9 %collective-permute-start = (f32[4,512,512]{2,1,0:T(8,128)}, f32[4,512,512]{2,1,0:T(8,128)}, u32[]{:S(2)}, u32[]{:S(2)}) collective-permute-start(f32[4,512,512]{2,1,0:T(8,128)} %pack.7), channel_id=1, source_target_pairs={{0,8},{1,9},{2,10},{3,11},{4,12},{5,13},{6,14},{7,15},{8,0},{9,1},... | collective-permute-start | bytes 12582920 | tf_op jit(solution)/shard_map/ppermute | solution.py:407
  35.5 101.4 %collective-permute-start.2 = (f32[4,512,512]{2,1,0:T(8,128)}, f32[4,512,512]{2,1,0:T(8,128)}, u32[]{:S(2)}, u32[]{:S(2)}) collective-permute-start(f32[4,512,512]{2,1,0:T(8,128)} %pack.9), channel_id=1, source_target_pairs={{0,1},{1,4},{2,3},{3,6},{8,9},{9,12},{10,11},{11,14},{20,17},{21,2... | collective-permute-start | bytes 12582920 | tf_op jit(solution)/shard_map/ppermute | solution.py:452
  48.1 95.6 %collective-permute-start.3 = (f32[4,512,512]{2,1,0:T(8,128)}, f32[4,512,512]{2,1,0:T(8,128)}, u32[]{:S(2)}, u32[]{:S(2)}) collective-permute-start(f32[4,512,512]{2,1,0:T(8,128)} %pack.10), channel_id=1, source_target_pairs={{0,2},{1,7},{2,0},{3,5},{8,10},{9,15},{10,8},{11,13},{20,18},{21,2... | collective-permute-start | bytes 12582920 | tf_op jit(solution)/shard_map/ppermute | solution.py:452
  57.5 86.3 %collective-permute-start.4 = (f32[4,512,512]{2,1,0:T(8,128)}, f32[4,512,512]{2,1,0:T(8,128)}, u32[]{:S(2)}, u32[]{:S(2)}) collective-permute-start(f32[4,512,512]{2,1,0:T(8,128)} %pack.11), channel_id=1, source_target_pairs={{0,3},{1,6},{2,1},{3,4},{8,11},{9,14},{10,9},{11,12},{20,19},{21,2... | collective-permute-start | bytes 12582920 | tf_op jit(solution)/shard_map/ppermute | solution.py:452
  79.4 76.9 %all-to-all-start.1 = ((f32[8,4,136,128]{3,2,1,0:T(8,128)}), f32[8,4,136,128]{3,2,1,0:T(8,128)}, u32[]{:S(2)}, u32[]{:S(2)}) async-start(f32[8,4,136,128]{3,2,1,0:T(8,128)} %select_select_fusion.2), calls=%async_computation.1 | async-start | bytes 4456448 | tf_op jit(solution)/shard_map/all_to_all | solution.py:437
  83.8 155.0 %all-gather.5.cloned.1.call-start = ((), (), s32[]{:S(2)}) async-start(), calls=%async_computation.3 | async-start | bytes 5242880 | tf_op jit(solution)/shard_map/all_gather | solution.py:459
  88.9 2.9 copy-start.1
  238.8 529.4 %all-to-all-start.2 = ((f32[8,2,512,512]{3,2,1,0:T(8,128)}), f32[8,2,512,512]{3,2,1,0:T(8,128)}, u32[]{:S(2)}, u32[]{:S(2)}) async-start(f32[8,2,512,512]{3,2,1,0:T(8,128)} %bitcast.97), calls=%async_computation.2 | async-start | bytes 33554432 | tf_op jit(solution)/shard_map/all_to_all | solution.py:494
  244.5 151.1 %all-gather.7.cloned.1.call-start = ((), (), s32[]{:S(2)}) async-start(), calls=%async_computation.4 | async-start | bytes 5242880 | tf_op jit(solution)/shard_map/all_gather | solution.py:463
  260.8 27.9 %collective-permute-start.5 = (f32[4,512,512]{2,1,0:T(8,128)}, f32[4,512,512]{2,1,0:T(8,128)}, u32[]{:S(2)}, u32[]{:S(2)}) collective-permute-start(f32[4,512,512]{2,1,0:T(8,128)} %pad_maximum_fusion.1), channel_id=1, source_target_pairs={{0,4},{1,5},{2,6},{3,7},{4,0},{5,1},{6,2},{7,3},{8,12},{9,13},{10,... | collective-permute-start | bytes 12582920 | tf_op jit(solution)/shard_map/ppermute | solution.py:486
  261.2 35.4 %collective-permute-start.6 = (f32[4,512,512]{2,1,0:T(8,128)}, f32[4,512,512]{2,1,0:T(8,128)}, u32[]{:S(2)}, u32[]{:S(2)}) collective-permute-start(f32[4,512,512]{2,1,0:T(8,128)} %bitcast.20.refs_0_), channel_id=1, source_target_pairs={{1,5},{11,15},{20,16},{30,26}} | collective-permute-start | bytes 12582920 | tf_op jit(solution)/shard_map/ppermute | solution.py:474
  263.8 51.1 %collective-permute-start.7 = (f32[4,512,512]{2,1,0:T(8,128)}, f32[4,512,512]{2,1,0:T(8,128)}, u32[]{:S(2)}, u32[]{:S(2)}) collective-permute-start(f32[4,512,512]{2,1,0:T(8,128)} %bitcast.20.refs_0_), channel_id=1, source_target_pairs={{0,1},{1,4},{10,11},{11,14},{20,17},{21,20},{30,27},{31,30}} | collective-permute-start | bytes 12582920 | tf_op jit(solution)/shard_map/ppermute | solution.py:474
  270.6 92.5 %collective-permute-start.8 = (f32[4,512,512]{2,1,0:T(8,128)}, f32[4,512,512]{2,1,0:T(8,128)}, u32[]{:S(2)}, u32[]{:S(2)}) collective-permute-start(f32[4,512,512]{2,1,0:T(8,128)} %bitcast.20.refs_0_), channel_id=1, source_target_pairs={{0,2},{1,7},{10,8},{11,13},{20,18},{21,23},{30,24},{31,29}} | collective-permute-start | bytes 12582920 | tf_op jit(solution)/shard_map/ppermute | solution.py:474
  273.9 89.3 %collective-permute-start.9 = (f32[4,512,512]{2,1,0:T(8,128)}, f32[4,512,512]{2,1,0:T(8,128)}, u32[]{:S(2)}, u32[]{:S(2)}) collective-permute-start(f32[4,512,512]{2,1,0:T(8,128)} %bitcast.20.refs_0_), channel_id=1, source_target_pairs={{0,3},{1,6},{10,9},{11,12},{20,19},{21,22},{30,25},{31,28}} | collective-permute-start | bytes 12582920 | tf_op jit(solution)/shard_map/ppermute | solution.py:474
  288.7 2.9 copy-start.3
  397.0 1.0 copy-start.2
  398.1 28.0 %collective-permute-start.11 = (f32[512,1024]{1,0:T(8,128)S(1)}, f32[512,1024]{1,0:T(8,128)}, u32[]{:S(2)}, u32[]{:S(2)}) collective-permute-start(f32[512,1024]{1,0:T(8,128)S(1)} %pad_maximum_fusion.3), channel_id=1, source_target_pairs={{0,1},{1,0},{8,9},{9,8},{16,17},{17,16},{24,25},{25,24}} | collective-permute-start | bytes 6291464 | tf_op jit(solution)/shard_map/ppermute | solution.py:499
  401.5 48.0 %collective-permute-start.12 = (f32[512,1024]{1,0:T(8,128)S(1)}, f32[512,1024]{1,0:T(8,128)}, u32[]{:S(2)}, u32[]{:S(2)}) collective-permute-start(f32[512,1024]{1,0:T(8,128)S(1)} %pad_maximum_fusion.3), channel_id=1, source_target_pairs={{0,2},{1,3},{8,10},{9,11},{16,18},{17,19},{24,26},{25,27}} | collective-permute-start | bytes 6291464 | tf_op jit(solution)/shard_map/ppermute | solution.py:499
  404.8 44.7 %collective-permute-start.13 = (f32[512,1024]{1,0:T(8,128)S(1)}, f32[512,1024]{1,0:T(8,128)}, u32[]{:S(2)}, u32[]{:S(2)}) collective-permute-start(f32[512,1024]{1,0:T(8,128)S(1)} %pad_maximum_fusion.3), channel_id=1, source_target_pairs={{0,3},{1,2},{8,11},{9,10},{16,19},{17,18},{24,27},{25,26}} | collective-permute-start | bytes 6291464 | tf_op jit(solution)/shard_map/ppermute | solution.py:499
  453.6 2.7 copy-start
  456.3 19.2 %collective-permute-start.14 = (f32[1024,1024]{1,0:T(8,128)}, f32[1024,1024]{1,0:T(8,128)}, u32[]{:S(2)}, u32[]{:S(2)}) collective-permute-start(f32[1024,1024]{1,0:T(8,128)} %pad_maximum_fusion.2), channel_id=1, source_target_pairs={{0,4},{1,5},{2,6},{3,7},{8,12},{9,13},{10,14},{11,15},{16,20},{17,... | collective-permute-start | bytes 12582920 | tf_op jit(solution)/shard_map/ppermute | solution.py:509
  459.6 103.2 %collective-permute-start.15 = (f32[4,512,512]{2,1,0:T(8,128)}, f32[4,512,512]{2,1,0:T(8,128)}, u32[]{:S(2)}, u32[]{:S(2)}) collective-permute-start(f32[4,512,512]{2,1,0:T(8,128)} %bitcast.25.refs_1_.refs_5_), channel_id=1, source_target_pairs={{1,5},{11,15},{20,16},{30,26}} | collective-permute-start | bytes 12582920 | tf_op jit(solution)/shard_map/ppermute | solution.py:474
  462.2 100.6 %collective-permute-start.16 = (f32[4,512,512]{2,1,0:T(8,128)}, f32[4,512,512]{2,1,0:T(8,128)}, u32[]{:S(2)}, u32[]{:S(2)}) collective-permute-start(f32[4,512,512]{2,1,0:T(8,128)} %bitcast.25.refs_1_.refs_5_), channel_id=1, source_target_pairs={{0,1},{1,4},{10,11},{11,14},{20,17},{21,20},{30,27},{31,30}} | collective-permute-start | bytes 12582920 | tf_op jit(solution)/shard_map/ppermute | solution.py:474
  468.2 94.6 %collective-permute-start.17 = (f32[4,512,512]{2,1,0:T(8,128)}, f32[4,512,512]{2,1,0:T(8,128)}, u32[]{:S(2)}, u32[]{:S(2)}) collective-permute-start(f32[4,512,512]{2,1,0:T(8,128)} %bitcast.25.refs_1_.refs_5_), channel_id=1, source_target_pairs={{0,2},{1,7},{10,8},{11,13},{20,18},{21,23},{30,24},{31,29}} | collective-permute-start | bytes 12582920 | tf_op jit(solution)/shard_map/ppermute | solution.py:474
  471.6 91.3 %collective-permute-start.18 = (f32[4,512,512]{2,1,0:T(8,128)}, f32[4,512,512]{2,1,0:T(8,128)}, u32[]{:S(2)}, u32[]{:S(2)}) collective-permute-start(f32[4,512,512]{2,1,0:T(8,128)} %bitcast.25.refs_1_.refs_5_), channel_id=1, source_target_pairs={{0,3},{1,6},{10,9},{11,12},{20,19},{21,22},{30,25},{31,28}} | collective-permute-start | bytes 12582920 | tf_op jit(solution)/shard_map/ppermute | solution.py:474
  589.0 69.7 %collective-permute-start.19 = (f32[4,512,1024]{2,1,0:T(8,128)}, f32[4,512,1024]{2,1,0:T(8,128)}, u32[]{:S(2)}, u32[]{:S(2)}) collective-permute-start(f32[4,512,1024]{2,1,0:T(8,128)} %solve.2.refs_2_), channel_id=1, source_target_pairs={{0,4},{1,5},{2,6},{3,7},{4,0},{5,1},{6,2},{7,3},{8,12},{9,13},{10,... | collective-permute-start | bytes 25165832 | tf_op jit(solution)/shard_map/ppermute | solution.py:545
  589.0 172.2 %collective-permute-start.10 = (f32[4,512,512]{2,1,0:T(8,128)}, f32[4,512,512]{2,1,0:T(8,128)}, u32[]{:S(2)}, u32[]{:S(2)}) collective-permute-start(f32[4,512,512]{2,1,0:T(8,128)} %get-tuple-element.54), channel_id=1, source_target_pairs={{0,8},{1,9},{2,10},{3,11},{4,12},{5,13},{6,14},{7,15},{8,0},{9,1},... | collective-permute-start | bytes 12582920 | tf_op jit(solution)/shard_map/ppermute | solution.py:514
Sparse Core Ops, SparseCore 0:
  156.4 82.3 all-gather.4
  246.9 148.6 all-gather.6
